TPU v7x, 256 devices: a whole 4x4x8 slice. The times are simulated.
256 devices in a mesh: row: 32 (over x_lo, z, core), col: 8 (over y, x_hi).
Axes of the slice: x: 4 (x_hi: 2, x_lo: 2; x = x_hi * 2 + x_lo), y: 4, z: 8, core: 2. Of those that a mesh axis runs over, the one named last changes fastest.
Arguments:
- features: bfloat16 [65536, 602], P(('row', 'col')), may hold values from -6 to 6
- weight: bfloat16 [602, 256], replicated, may hold values from -0.25 to 0.25
- adj_tiles: bfloat16 [32, 8, 32, 6, 128, 128], P('row', 'col'), may hold values from 0.00077819824 to 0.03125
- tile_row: int32 [32, 8, 32, 6], P('row', 'col'), may hold values from 0 to 15, as said below
- tile_col: int32 [32, 8, 32, 6], P('row', 'col'), may hold values from 0 to 1
- tile_count: int32 [32, 8, 32], P('row', 'col'), may hold values from 1 to 6, as said below
- train_mask: int32 [65536], P(('row', 'col')), may hold values 0 or 1
- cotangent: bfloat16 [65536, 256], P(('row', 'col')), may hold values from -6 to 6
Outputs:
- hidden: bfloat16 [65536, 256], P(('row', 'col'))
- grad_features: bfloat16 [65536, 602], P(('row', 'col'))
- grad_weight: float32 [602, 256], replicated
Inputs may be any that keep to these rules, and one draw needn't show every extreme that they name: For each [r, c, j], the pairs (tile_row, tile_col) of the slots are distinct. tile_count[r, c, r] = 6 for every r and c.
All inputs are finite; a program needn't handle non-finite values. No bound on the sum of `train_mask` on one device may be relied on, other than what follows from the above.
Results may differ from a plain program's by a relative error of at most 0.0075.
Values may be sent and summed in bfloat16 or wider, within the bound.
No kernel may reach another device: no remote copies, remote signals or barrier semaphores. Data moves between devices by JAX's collectives and lax.ppermute only.
A program may use at most 128 MiB of HBM per device.

v0:
```python
import functools
import math

import jax
import jax.numpy as jnp
import numpy as np
from jax import lax
from jax.experimental import pallas as pl
from jax.experimental.pallas import tpu as pltpu
from jax.sharding import PartitionSpec as P

ROWS, COLS, ZS = 32, 8, 8
BF, F32 = jnp.bfloat16, jnp.float32
UP_DOWN = [0, -1, 1, -2, 2, -3, 3, 4]
FAR_FIRST = [4, -3, 3, -2, 2, -1, 1, 0]
VMEM = 60 << 20
WEIGHT_ROWS = 640

CORE = [(i, i ^ 1) for i in range(ROWS)]
XLO = [(i, i ^ 16) for i in range(ROWS)]
XHI = [(i, i ^ 1) for i in range(COLS)]


def ring_z(step):
    return [(i, (i // 16) * 16 + (i % 16 + 2 * step) % 16) for i in range(ROWS)]


def ring_y(step):
    return [(i, (i + 2 * step) % COLS) for i in range(COLS)]


def to_row(value, route):
    return lax.ppermute(value, "row", route)


def to_col(value, route):
    return lax.ppermute(value, "col", route)


def masked_tiles(tiles, cols, first):
    placed = []
    for s in range(tiles.shape[0]):
        tile, where = tiles[s], cols[first + s]
        zero = jnp.zeros_like(tile)
        placed.append(
            jnp.concatenate([jnp.where(where == 0, tile, zero), jnp.where(where == 1, tile, zero)], axis=1)
        )
    return jnp.concatenate(placed, axis=0)


def forward_kernel(base, half, fresh, last, blocks, rows, cols, adj, *refs):
    pairs, (held, tiles, total, held_sems, tile_sems, total_sem) = refs[:half], refs[-6:]
    outs = refs[half + (0 if fresh else 1) : -6]
    slots = tiles.shape[1]
    for q in range(half):
        if not last:
            pltpu.make_async_copy(pairs[q], held.at[q], held_sems.at[q]).start()
        for k in (2 * q, 2 * q + 1):
            pltpu.make_async_copy(adj.at[blocks[base + k]], tiles.at[k], tile_sems.at[k]).start()
    if fresh:
        total[...] = jnp.zeros_like(total)
    else:
        carried = pltpu.make_async_copy(refs[half], total, total_sem)
        carried.start()

    def step(q, _):
        if not last:
            pltpu.make_async_copy(pairs[0], held.at[q], held_sems.at[q]).wait()
        for k in (2 * q, 2 * q + 1):
            pltpu.make_async_copy(adj.at[0], tiles.at[k], tile_sems.at[k]).wait()
        products = []
        for far in range(2):
            k = 2 * q + far
            lhs = masked_tiles(tiles.at[k], cols, blocks[base + k] * slots)
            products.append(jnp.dot(lhs, pairs[q][far] if last else held[q, far], preferred_element_type=F32))
        if last and q == 0:
            carried.wait()
        for far in range(2):
            first = blocks[base + 2 * q + far] * slots
            for s in range(slots):
                total[rows[first + s]] += products[far][s * 128 : (s + 1) * 128]
        return 0

    if last:
        for q in range(half):
            step(q, 0)
    else:
        lax.fori_loop(0, half, step, 0)
        carried = pltpu.make_async_copy(total, outs[0], total_sem)
        carried.start()
        carried.wait()
        return
    outs[0][...] = total[:2].reshape(256, 256)
    for p in range(1, COLS):
        outs[p][...] = total[2 * p : 2 * p + 2].reshape(256, 256).astype(BF)


def forward_part(adj, rows, cols, blocks, base, pairs, total, last):
    slots, half = adj.shape[1], len(pairs)
    smem, hbm = pl.BlockSpec(memory_space=pltpu.SMEM), pl.BlockSpec(memory_space=pltpu.HBM)
    vmem = pl.BlockSpec(memory_space=pltpu.VMEM)
    operands = list(pairs) + ([] if total is None else [total])
    if last:
        shapes = [jax.ShapeDtypeStruct((256, 256), F32 if p == 0 else BF) for p in range(COLS)]
    else:
        shapes = [jax.ShapeDtypeStruct((16, 128, 256), F32)]
    outs = pl.pallas_call(
        functools.partial(forward_kernel, base, half, total is None, last),
        in_specs=[smem] * 3 + [hbm] + [vmem if last else hbm] * half + [hbm] * (len(operands) - half),
        out_specs=[vmem if last else hbm] * len(shapes),
        out_shape=shapes,
        scratch_shapes=[
            pltpu.VMEM((half, 2, 256, 256), BF),
            pltpu.VMEM((2 * half, slots, 128, 128), BF),
            pltpu.VMEM((16, 128, 256), F32),
            pltpu.SemaphoreType.DMA((half,)),
            pltpu.SemaphoreType.DMA((2 * half,)),
            pltpu.SemaphoreType.DMA,
        ],
        cost_estimate=pl.CostEstimate(
            flops=4 * half * 768 * 256 * 256, bytes_accessed=half * (1 << 20) + (1 << 22), transcendentals=0
        ),
        compiler_params=pltpu.CompilerParams(vmem_limit_bytes=VMEM),
    )(blocks, rows, cols, adj, *operands)
    return outs if last else outs[0]


def backward_kernel(base, blocks, rows, cols, adj, grads, out, tiles, sems):
    count, slots = tiles.shape[:2]
    for k in range(count):
        pltpu.make_async_copy(adj.at[blocks[base + k]], tiles.at[k], sems.at[k]).start()

    def step(q, _):
        for k in (2 * q, 2 * q + 1):
            pltpu.make_async_copy(adj.at[0], tiles.at[k], sems.at[k]).wait()
        for k in (2 * q, 2 * q + 1):
            first = blocks[base + k] * slots
            rhs = masked_tiles(tiles.at[k], cols, first)
            lhs = jnp.concatenate([grads[rows[first + s]] for s in range(slots)], axis=1)
            product = jnp.dot(lhs, rhs, preferred_element_type=F32)
            out[k] = product.astype(BF)
        return 0

    lax.fori_loop(0, count // 2, step, 0)


def backward_part(adj, rows, cols, blocks, base, count, grads):
    slots = adj.shape[1]
    smem, vmem = pl.BlockSpec(memory_space=pltpu.SMEM), pl.BlockSpec(memory_space=pltpu.VMEM)
    return pl.pallas_call(
        functools.partial(backward_kernel, base),
        in_specs=[smem] * 3 + [pl.BlockSpec(memory_space=pltpu.HBM)] + [vmem],
        out_specs=vmem,
        out_shape=jax.ShapeDtypeStruct((count, 256, 256), BF),
        scratch_shapes=[pltpu.VMEM((count, slots, 128, 128), BF), pltpu.SemaphoreType.DMA((count,))],
        cost_estimate=pl.CostEstimate(
            flops=2 * count * 768 * 256 * 256, bytes_accessed=count * (1 << 19) + (1 << 20), transcendentals=0
        ),
        compiler_params=pltpu.CompilerParams(vmem_limit_bytes=VMEM),
    )(blocks, rows, cols, adj, grads)


def sum_everywhere(value, core, beside):
    halves = value.reshape(2, 320, 256)
    mine = jnp.where(core == 0, halves[0], halves[1])
    other = jnp.where(core == 0, halves[1], halves[0])
    part = mine + to_row(other, CORE)
    part = jnp.sum(lax.all_to_all(part.reshape(COLS, 40, 256), "col", 0, 0), axis=0)
    part, beside = lax.optimization_barrier((part, beside))
    groups = [[2 * i + c for i in range(ROWS // 2)] for c in range(2)]
    every = jnp.broadcast_to(part.astype(BF)[None], (ROWS // 2,) + part.shape)
    every = lax.all_to_all(every, "row", 0, 0, axis_index_groups=groups)
    part = jnp.sum(every.astype(F32), axis=0)
    every = lax.all_to_all(jnp.broadcast_to(part[None], (COLS,) + part.shape), "col", 0, 0)
    part = every.reshape(320, 256)
    other = to_row(part, CORE)
    low = jnp.where(core == 0, part, other)
    high = jnp.where(core == 0, other, part)
    return jnp.concatenate([low, high], axis=0), beside


def body(features, weight, adj_tiles, tile_row, tile_col, tile_count, train_mask, cotangent):
    row, col = lax.axis_index("row"), lax.axis_index("col")
    core, z, x_lo = row % 2, (row // 2) % ZS, row // 16
    y, x_hi = col // 2, col % 2
    adj = adj_tiles[0, 0]
    slots = adj.shape[1]
    live = jnp.arange(slots)[None, :] < tile_count[0, 0][:, None]
    cols = jnp.where(live, tile_col[0, 0], 2).reshape(-1)
    rows = tile_row[0, 0].reshape(-1)
    owner = rows // 2
    near = (((owner // 2 - y) % 4) * 2 + (owner % 2 ^ x_hi)) * 2 + rows % 2

    forward_order = [(d, far, across) for d in UP_DOWN for across in (0, 1) for far in (0, 1)]
    backward_order = [(d, far, across) for across in (1, 0) for d in FAR_FIRST for far in (0, 1)]
    d, far, across = (jnp.asarray(v, jnp.int32) for v in np.array(forward_order + backward_order).T)
    blocks = (x_lo ^ far) * 16 + ((z + d) % ZS) * 2 + (core ^ across)

    projected = jnp.dot(features, weight, preferred_element_type=F32).astype(BF)
    pair = jnp.stack([projected, to_row(projected, XLO)])

    up = down = pair
    pairs = [pair, to_row(pair, CORE)]
    for k in range(1, 4):
        up, down = to_row(up, ring_z(1)), to_row(down, ring_z(-1))
        if k == 1:
            up, blocks, near, cols = lax.optimization_barrier((up, blocks, near, cols))
        pairs += [up, to_row(up, CORE), down, to_row(down, CORE)]
    up = to_row(up, ring_z(1))
    total = forward_part(adj, near, cols, blocks, 0, pairs, None, False)
    up, total = lax.optimization_barrier((up, total))
    parts = forward_part(adj, near, cols, blocks, 28, [up, to_row(up, CORE)], total, True)

    pre_act = parts[0]
    for d, far in ((2, 1), (2, 0), (1, 1), (1, 0), (3, 1), (3, 0), (0, 1)):
        route = [(i, (i + 2 * d) % COLS ^ far) for i in range(COLS)]
        pre_act = pre_act + to_col(parts[2 * d + far], route).astype(F32)
    gate = jax.nn.sigmoid(pre_act)
    hidden = (pre_act * gate).astype(BF)
    grad_pre = (
        cotangent.astype(F32) * train_mask.astype(F32)[:, None] * gate * (1.0 + pre_act * (1.0 - gate))
    ).astype(BF)

    mine = jnp.swapaxes(grad_pre.reshape(2, 128, 256), 1, 2)
    across_x = to_col(mine, XHI)
    pieces = [mine, across_x] + [None] * 6
    for d in (1, 3, 2):
        pieces[2 * d] = to_col(mine, ring_y(-d))
    for d in (1, 3, 2):
        pieces[2 * d + 1] = to_col(across_x, ring_y(-d))
    grads = jnp.concatenate(pieces, axis=0)

    theirs = backward_part(adj, near, cols, blocks, 32, 16, grads)
    theirs, grads = lax.optimization_barrier((theirs, grads))
    theirs = to_row(theirs, CORE)
    ours = backward_part(adj, near, cols, blocks, 48, 16, grads)

    def add(d, *arrived):
        k = 2 * FAR_FIRST.index(d)
        total = ours[k : k + 2].astype(F32) + theirs[k : k + 2].astype(F32)
        for value in arrived:
            total = total + value.astype(F32)
        return total

    up, down = lax.optimization_barrier((add(4).astype(BF), add(-3).astype(BF)))
    up, down = to_row(up, ring_z(1)), to_row(down, ring_z(-1))
    features_t = features.T
    for k in (3, 2, 1):
        up, down = add(k, up).astype(BF), (add(1 - k, down).astype(BF) if k > 1 else down)
        up, down = lax.optimization_barrier((up, down))
        up, down = to_row(up, ring_z(1)), (to_row(down, ring_z(-1)) if k > 1 else down)
        if k == 2:
            features_x = to_row(features_t, XLO)
    both = add(0, up, down)
    across_x = both[1].astype(BF)

    grad_scale = 1.0 / math.sqrt(ROWS * COLS * features.shape[0])
    local_grad = lax.dot_general(
        jnp.concatenate([features_t, features_x], axis=1),
        jnp.concatenate([both[0].astype(BF), across_x], axis=1),
        (((1,), (1,)), ((), ())),
        preferred_element_type=F32,
    )
    local_grad = jnp.pad(local_grad * grad_scale, ((0, WEIGHT_ROWS - features.shape[1]), (0, 0)))
    grad_proj = (both[0] + to_row(across_x, XLO).astype(F32)).astype(BF)
    grad_features = lax.dot_general(
        grad_proj, weight, (((0,), (1,)), ((), ())), preferred_element_type=F32
    ).astype(BF)
    grad_weight, grad_features = sum_everywhere(local_grad, core, grad_features)
    return (hidden, grad_features, grad_weight[: features.shape[1]])


def solution(mesh):
    in_specs = (
        P(("row", "col"), None),
        P(),
        P("row", "col", None, None, None, None),
        P("row", "col", None, None),
        P("row", "col", None, None),
        P("row", "col", None),
        P(("row", "col")),
        P(("row", "col"), None),
    )
    out_specs = (P(("row", "col"), None), P(("row", "col"), None), P())
    return jax.shard_map(body, mesh=mesh, in_specs=in_specs, out_specs=out_specs, check_vma=False)
```

profile of v0, /device:TPU:1, one launch (start us, length us, event | category | flops | bytes accessed | tf_op | source)
XLA Modules:
  0.0 204.9 jit_solution(8808958911057453740)
XLA Ops:
  9.9 4.0 %collective-permute-start.7 = (bf16[2,256,256]{2,1,0:T(8,128)(2,1)S(1)}, bf16[2,256,256]{2,1,0:T(8,128)(2,1)S(1)}, u32[]{:S(2)}, u32[]{:S(2)}) collective-permute-start(bf16[2,256,256]{2,1,0:T(8,128)(2,1)S(1)} %pad_maximum_fusion.1.refs_0_), channel_id=1, source_target_pairs={{0,112},{8,120},{16,0},{24,8},{32,16},{40,24},{48,32},{56,40},{64,... | collective-permute-start | bytes 786440 | tf_op jit(solution)/shard_map/ppermute | solution.py:33
  21.6 2.7 %collective-permute-start.5 = (bf16[2,256,256]{2,1,0:T(8,128)(2,1)S(1)}, bf16[2,256,256]{2,1,0:T(8,128)(2,1)S(1)}, u32[]{:S(2)}, u32[]{:S(2)}) collective-permute-start(bf16[2,256,256]{2,1,0:T(8,128)(2,1)S(1)} %pad_maximum_fusion.1.refs_0_), channel_id=1, source_target_pairs={{0,8},{8,0},{16,24},{24,16},{32,40},{40,32},{48,56},{56,48},{64,72... | collective-permute-start | bytes 786440 | tf_op jit(solution)/shard_map/ppermute | solution.py:33
  28.4 3.7 %collective-permute-start.8 = (bf16[2,256,256]{2,1,0:T(8,128)(2,1)S(1)}, bf16[2,256,256]{2,1,0:T(8,128)(2,1)S(1)}, u32[]{:S(2)}, u32[]{:S(2)}) collective-permute-start(bf16[2,256,256]{2,1,0:T(8,128)(2,1)S(1)} %collective-permute-done.7.refs_4_), channel_id=1, source_target_pairs={{0,8},{8,0},{16,24},{24,16},{32,40},{40,32},{48,56},{56,48},{64,72... | collective-permute-start | bytes 786440 | tf_op jit(solution)/shard_map/ppermute | solution.py:33
  32.6 3.8 %collective-permute-start.12 = (bf16[2,256,256]{2,1,0:T(8,128)(2,1)S(1)}, bf16[2,256,256]{2,1,0:T(8,128)(2,1)S(1)}, u32[]{:S(2)}, u32[]{:S(2)}) collective-permute-start(bf16[2,256,256]{2,1,0:T(8,128)(2,1)S(1)} %collective-permute-done.3.refs_10_), channel_id=1, source_target_pairs={{0,8},{8,0},{16,24},{24,16},{32,40},{40,32},{48,56},{56,48},{64,72... | collective-permute-start | bytes 786440 | tf_op jit(solution)/shard_map/ppermute | solution.py:33
  38.8 10.5 %shard_map.130.refs_2_ = f32[16,128,256]{2,1,0:T(8,128)} custom-call(s32[64]{0:T(128)} %fusion.16.blocks, s32[192]{0:T(256)} %get-tuple-element.30.rows, s32[192]{0:T(256)} %get-tuple-element.31.cols, bf16[32,6,128,128]{3,2,1,0:T(8,128)(2,1)} %bitcast.28, bf16[2,256,256]{2,1,0:T(8,128)(2,1)} %copy-done.3, bf16[2,256,256]{2,1,0:T(8,128)(2,1)} %copy-done.8, ...), custom_call_target="tpu_custom_call" | custom-call | flops 2818572288 | bytes 18874368 | tf_op jit(solution)/shard_map/pallas_call | solution.py:107
  51.9 4.7 %shard_map.131 = (f32[256,256]{1,0:T(8,128)}, bf16[256,256]{1,0:T(8,128)(2,1)}, bf16[256,256]{1,0:T(8,128)(2,1)}, bf16[256,256]{1,0:T(8,128)(2,1)}, bf16[256,256...) custom-call(s32[64]{0:T(128)} %fusion.16.blocks, ...), custom_call_target="tpu_custom_call" | custom-call | flops 402653184 | bytes 6291456 | tf_op jit(solution)/shard_map/pallas_call | solution.py:107
  56.6 2.8 %collective-permute-start.22 = (bf16[256,256]{1,0:T(8,128)(2,1)}, bf16[256,256]{1,0:T(8,128)(2,1)S(1)}, u32[]{:S(2)}, u32[]{:S(2)}) collective-permute-start(bf16[256,256]{1,0:T(8,128)(2,1)} %get-tuple-element.42), channel_id=1, source_target_pairs={{0,1},{1,0},{2,3},{3,2},{4,5},{5,4},{6,7},{7,6},{8,9},{9,8},{10,11... | collective-permute-start | bytes 393224 | tf_op jit(solution)/shard_map/ppermute | solution.py:37
  66.1 2.9 %collective-permute-start.17 = (bf16[256,256]{1,0:T(8,128)(2,1)}, bf16[256,256]{1,0:T(8,128)(2,1)S(1)}, u32[]{:S(2)}, u32[]{:S(2)}) collective-permute-start(bf16[256,256]{1,0:T(8,128)(2,1)} %get-tuple-element.37), channel_id=1, source_target_pairs={{0,4},{1,5},{2,6},{3,7},{4,0},{5,1},{6,2},{7,3},{8,12},{9,13},{10,... | collective-permute-start | bytes 393224 | tf_op jit(solution)/shard_map/ppermute | solution.py:37
  71.3 3.9 %collective-permute-done.17 = bf16[256,256]{1,0:T(8,128)(2,1)S(1)} collective-permute-done((bf16[256,256]{1,0:T(8,128)(2,1)}, bf16[256,256]{1,0:T(8,128)(2,1)S(1)}, u32[]{:S(2)}, u32[]{:S(2)}) %collective-permute-start.17) | collective-permute-done | bytes 131104 | tf_op jit(solution)/shard_map/ppermute | solution.py:37
  79.5 3.7 %collective-permute-start.27 = (bf16[2,256,128]{2,1,0:T(8,128)(2,1)S(1)}, bf16[2,256,128]{2,1,0:T(8,128)(2,1)S(1)}, u32[]{:S(2)}, u32[]{:S(2)}) collective-permute-start(bf16[2,256,128]{2,1,0:T(8,128)(2,1)S(1)} %bitcast.36), channel_id=1, source_target_pairs={{0,4},{1,5},{2,6},{3,7},{4,0},{5,1},{6,2},{7,3},{8,12},{9,13},{10,... | collective-permute-start | bytes 393224 | tf_op jit(solution)/shard_map/ppermute | solution.py:37
  86.6 3.6 %collective-permute-done.26 = bf16[2,256,128]{2,1,0:T(8,128)(2,1)S(1)} collective-permute-done((bf16[2,256,128]{2,1,0:T(8,128)(2,1)S(1)}, bf16[2,256,128]{2,1,0:T(8,128)(2,1)S(1)}, u32[]{:S(2)}, u32[]{:S(2)}) %collective-permute-start.26) | collective-permute-done | bytes 131104 | tf_op jit(solution)/shard_map/ppermute | solution.py:37
  96.2 6.8 %shard_map.132 = bf16[16,256,256]{2,1,0:T(8,128)(2,1)} custom-call(s32[64]{0:T(128)} %fusion.16.blocks, s32[192]{0:T(256)} %get-tuple-element.30.rows, s32[192]{0:T(256)} %get-tuple-element.31.cols, bf16[32,6,128,128]{3,2,1,0:T(8,128)(2,1)} %bitcast.30, bf16[16,256,128]{2,1,0:T(8,128)(2,1)} %copy-done.2), custom_call_target="tpu_custom_call" | custom-call | flops 1610612736 | bytes 9437184 | tf_op jit(solution)/shard_map/pallas_call | solution.py:150
  105.5 6.8 %shard_map.133 = bf16[16,256,256]{2,1,0:T(8,128)(2,1)} custom-call(s32[64]{0:T(128)} %fusion.16.blocks, s32[192]{0:T(256)} %get-tuple-element.30.rows, s32[192]{0:T(256)} %get-tuple-element.31.cols, bf16[32,6,128,128]{3,2,1,0:T(8,128)(2,1)} %bitcast.31, bf16[16,256,128]{2,1,0:T(8,128)(2,1)} %copy-done.2), custom_call_target="tpu_custom_call" | custom-call | flops 1610612736 | bytes 9437184 | tf_op jit(solution)/shard_map/pallas_call | solution.py:150
  116.5 5.7 %collective-permute-done.33 = bf16[2,256,256]{2,1,0:T(8,128)(2,1)S(1)} collective-permute-done((bf16[2,256,256]{2,1,0:T(8,128)(2,1)S(1)}, bf16[2,256,256]{2,1,0:T(8,128)(2,1)S(1)}, u32[]{:S(2)}, u32[]{:S(2)}) %collective-permute-start.33) | collective-permute-done | bytes 262176 | tf_op jit(solution)/shard_map/ppermute | solution.py:33
  122.2 3.1 %collective-permute-done.32 = bf16[2,256,256]{2,1,0:T(8,128)(2,1)S(1)} collective-permute-done((bf16[2,256,256]{2,1,0:T(8,128)(2,1)S(1)}, bf16[2,256,256]{2,1,0:T(8,128)(2,1)S(1)}, u32[]{:S(2)}, u32[]{:S(2)}) %collective-permute-start.32) | collective-permute-done | bytes 262176 | tf_op jit(solution)/shard_map/ppermute | solution.py:33
  128.2 5.2 %collective-permute-done.35 = bf16[2,256,256]{2,1,0:T(8,128)(2,1)S(1)} collective-permute-done((bf16[2,256,256]{2,1,0:T(8,128)(2,1)S(1)}, bf16[2,256,256]{2,1,0:T(8,128)(2,1)S(1)}, u32[]{:S(2)}, u32[]{:S(2)}) %collective-permute-start.35) | collective-permute-done | bytes 262176 | tf_op jit(solution)/shard_map/ppermute | solution.py:33
  139.0 4.3 %collective-permute-done.36 = bf16[2,256,256]{2,1,0:T(8,128)(2,1)S(1)} collective-permute-done((bf16[2,256,256]{2,1,0:T(8,128)(2,1)S(1)}, bf16[2,256,256]{2,1,0:T(8,128)(2,1)S(1)}, u32[]{:S(2)}, u32[]{:S(2)}) %collective-permute-start.36) | collective-permute-done | bytes 262176 | tf_op jit(solution)/shard_map/ppermute | solution.py:33
  145.2 5.8 %collective-permute-done.38 = bf16[2,256,256]{2,1,0:T(8,128)(2,1)} collective-permute-done((bf16[2,256,256]{2,1,0:T(8,128)(2,1)S(1)}, bf16[2,256,256]{2,1,0:T(8,128)(2,1)}, u32[]{:S(2)}, u32[]{:S(2)}) %collective-permute-start.38) | collective-permute-done | bytes 262176 | tf_op jit(solution)/shard_map/ppermute | solution.py:33
  153.7 4.2 %collective-permute-start.39 = (f32[320,256]{1,0:T(8,128)S(1)}, f32[320,256]{1,0:T(8,128)S(1)}, u32[]{:S(2)}, u32[]{:S(2)}) collective-permute-start(f32[320,256]{1,0:T(8,128)S(1)} %slice_select_fusion), channel_id=1, source_target_pairs={{0,8},{8,0},{16,24},{24,16},{32,40},{40,32},{48,56},{56,48},{64,72... | collective-permute-start | bytes 983048 | tf_op jit(solution)/shard_map/ppermute | solution.py:33
  159.9 4.0 %all-to-all-start = ((f32[8,40,256]{2,1,0:T(8,128)}), f32[8,40,256]{2,1,0:T(8,128)S(1)}, u32[]{:S(2)}, u32[]{:S(2)}) async-start(f32[8,40,256]{2,1,0:T(8,128)} %bitcast.9), calls=%async_computation | async-start | bytes 655360 | tf_op jit(solution)/shard_map/all_to_all | solution.py:168
  164.8 7.9 %all-to-all-done = f32[8,40,256]{2,1,0:T(8,128)S(1)} async-done(((f32[8,40,256]{2,1,0:T(8,128)}), f32[8,40,256]{2,1,0:T(8,128)S(1)}, u32[]{:S(2)}, u32[]{:S(2)}) %all-to-all-start) | async-done | bytes 327712 | tf_op jit(solution)/shard_map/all_to_all | solution.py:168
  172.8 13.8 %all_to_all.15 = bf16[16,40,256]{2,1,0:T(8,128)(2,1)S(1)} all-to-all(bf16[16,40,256]{2,1,0:T(8,128)(2,1)S(1)} %broadcast_in_dim.6), channel_id=1, replica_groups={{0,16,32,48,64,80,96,112,128,144,160,176,192,208,224,240},{8,24,40,56,7..., dimensions={0} | all-to-all | bytes 655360 | tf_op jit(solution)/shard_map/all_to_all | solution.py:172
  186.8 11.5 %all_to_all.16 = f32[8,40,256]{2,1,0:T(8,128)S(1)} all-to-all(f32[8,40,256]{2,1,0:T(8,128)S(1)} %broadcast_in_dim.7), channel_id=1, replica_groups=mesh['row'=32,'col'=8] {'col'}, dimensions={0} | all-to-all | bytes 655360 | tf_op jit(solution)/shard_map/all_to_all | solution.py:174
  198.3 4.5 %collective-permute-start.41 = (f32[320,256]{1,0:T(8,128)S(1)}, f32[320,256]{1,0:T(8,128)S(1)}, u32[]{:S(2)}, u32[]{:S(2)}) collective-permute-start(f32[320,256]{1,0:T(8,128)S(1)} %bitcast.32), channel_id=1, source_target_pairs={{0,8},{8,0},{16,24},{24,16},{32,40},{40,32},{48,56},{56,48},{64,72... | collective-permute-start | bytes 983048 | tf_op jit(solution)/shard_map/ppermute | solution.py:33
  (148 shorter events, 73.7 us)
Async XLA Ops:
  7.4 11.5 %collective-permute-start.1 = (bf16[2,256,256]{2,1,0:T(8,128)(2,1)S(1)}, bf16[2,256,256]{2,1,0:T(8,128)(2,1)S(1)}, u32[]{:S(2)}, u32[]{:S(2)}) collective-permute-start(bf16[2,256,256]{2,1,0:T(8,128)(2,1)S(1)} %pad_maximum_fusion.1.refs_0_), channel_id=1, source_target_pairs={{0,16},{8,24},{16,32},{24,40},{32,48},{40,56},{48,64},{56,72},{64,... | collective-permute-start | bytes 786440 | tf_op jit(solution)/shard_map/ppermute | solution.py:33
  9.9 9.0 %collective-permute-start.7 = (bf16[2,256,256]{2,1,0:T(8,128)(2,1)S(1)}, bf16[2,256,256]{2,1,0:T(8,128)(2,1)S(1)}, u32[]{:S(2)}, u32[]{:S(2)}) collective-permute-start(bf16[2,256,256]{2,1,0:T(8,128)(2,1)S(1)} %pad_maximum_fusion.1.refs_0_), channel_id=1, source_target_pairs={{0,112},{8,120},{16,0},{24,8},{32,16},{40,24},{48,32},{56,40},{64,... | collective-permute-start | bytes 786440 | tf_op jit(solution)/shard_map/ppermute | solution.py:33
  21.6 10.5 %collective-permute-start.5 = (bf16[2,256,256]{2,1,0:T(8,128)(2,1)S(1)}, bf16[2,256,256]{2,1,0:T(8,128)(2,1)S(1)}, u32[]{:S(2)}, u32[]{:S(2)}) collective-permute-start(bf16[2,256,256]{2,1,0:T(8,128)(2,1)S(1)} %pad_maximum_fusion.1.refs_0_), channel_id=1, source_target_pairs={{0,8},{8,0},{16,24},{24,16},{32,40},{40,32},{48,56},{56,48},{64,72... | collective-permute-start | bytes 786440 | tf_op jit(solution)/shard_map/ppermute | solution.py:33
  24.4 7.8 %collective-permute-start.6 = (bf16[2,256,256]{2,1,0:T(8,128)(2,1)S(1)}, bf16[2,256,256]{2,1,0:T(8,128)(2,1)S(1)}, u32[]{:S(2)}, u32[]{:S(2)}) collective-permute-start(bf16[2,256,256]{2,1,0:T(8,128)(2,1)S(1)} %collective-permute-done.1.refs_2_), channel_id=1, source_target_pairs={{0,8},{8,0},{16,24},{24,16},{32,40},{40,32},{48,56},{56,48},{64,72... | collective-permute-start | bytes 786440 | tf_op jit(solution)/shard_map/ppermute | solution.py:33
  25.8 6.9 %collective-permute-start.3 = (bf16[2,256,256]{2,1,0:T(8,128)(2,1)S(1)}, bf16[2,256,256]{2,1,0:T(8,128)(2,1)S(1)}, u32[]{:S(2)}, u32[]{:S(2)}) collective-permute-start(bf16[2,256,256]{2,1,0:T(8,128)(2,1)S(1)} %collective-permute-done.2.refs_6_), channel_id=1, source_target_pairs={{0,16},{8,24},{16,32},{24,40},{32,48},{40,56},{48,64},{56,72},{64,... | collective-permute-start | bytes 786440 | tf_op jit(solution)/shard_map/ppermute | solution.py:33
  25.8 10.7 %collective-permute-start.13 = (bf16[2,256,256]{2,1,0:T(8,128)(2,1)S(1)}, bf16[2,256,256]{2,1,0:T(8,128)(2,1)S(1)}, u32[]{:S(2)}, u32[]{:S(2)}) collective-permute-start(bf16[2,256,256]{2,1,0:T(8,128)(2,1)S(1)} %collective-permute-done.10.refs_8_), channel_id=1, source_target_pairs={{0,112},{8,120},{16,0},{24,8},{32,16},{40,24},{48,32},{56,40},{64,... | collective-permute-start | bytes 786440 | tf_op jit(solution)/shard_map/ppermute | solution.py:33
  28.4 8.1 %collective-permute-start.8 = (bf16[2,256,256]{2,1,0:T(8,128)(2,1)S(1)}, bf16[2,256,256]{2,1,0:T(8,128)(2,1)S(1)}, u32[]{:S(2)}, u32[]{:S(2)}) collective-permute-start(bf16[2,256,256]{2,1,0:T(8,128)(2,1)S(1)} %collective-permute-done.7.refs_4_), channel_id=1, source_target_pairs={{0,8},{8,0},{16,24},{24,16},{32,40},{40,32},{48,56},{56,48},{64,72... | collective-permute-start | bytes 786440 | tf_op jit(solution)/shard_map/ppermute | solution.py:33
  36.6 12.8 %collective-permute-start.4 = (bf16[2,256,256]{2,1,0:T(8,128)(2,1)S(1)}, bf16[2,256,256]{2,1,0:T(8,128)(2,1)S(1)}, u32[]{:S(2)}, u32[]{:S(2)}) collective-permute-start(bf16[2,256,256]{2,1,0:T(8,128)(2,1)S(1)} %collective-permute-done.3.refs_10_), channel_id=1, source_target_pairs={{0,16},{8,24},{16,32},{24,40},{32,48},{40,56},{48,64},{56,72},{64,... | collective-permute-start | bytes 786440 | tf_op jit(solution)/shard_map/ppermute | solution.py:33
  56.6 9.4 %collective-permute-start.22 = (bf16[256,256]{1,0:T(8,128)(2,1)}, bf16[256,256]{1,0:T(8,128)(2,1)S(1)}, u32[]{:S(2)}, u32[]{:S(2)}) collective-permute-start(bf16[256,256]{1,0:T(8,128)(2,1)} %get-tuple-element.42), channel_id=1, source_target_pairs={{0,1},{1,0},{2,3},{3,2},{4,5},{5,4},{6,7},{7,6},{8,9},{9,8},{10,11... | collective-permute-start | bytes 393224 | tf_op jit(solution)/shard_map/ppermute | solution.py:37
  59.5 9.5 %collective-permute-start.21 = (bf16[256,256]{1,0:T(8,128)(2,1)}, bf16[256,256]{1,0:T(8,128)(2,1)S(1)}, u32[]{:S(2)}, u32[]{:S(2)}) collective-permute-start(bf16[256,256]{1,0:T(8,128)(2,1)} %get-tuple-element.41), channel_id=1, source_target_pairs={{0,6},{1,7},{2,0},{3,1},{4,2},{5,3},{6,4},{7,5},{8,14},{9,15},{10,... | collective-permute-start | bytes 393224 | tf_op jit(solution)/shard_map/ppermute | solution.py:37
  63.6 7.7 %collective-permute-start.18 = (bf16[256,256]{1,0:T(8,128)(2,1)}, bf16[256,256]{1,0:T(8,128)(2,1)S(1)}, u32[]{:S(2)}, u32[]{:S(2)}) collective-permute-start(bf16[256,256]{1,0:T(8,128)(2,1)} %get-tuple-element.38), channel_id=1, source_target_pairs={{0,3},{1,2},{2,5},{3,4},{4,7},{5,6},{6,1},{7,0},{8,11},{9,10},{10,... | collective-permute-start | bytes 393224 | tf_op jit(solution)/shard_map/ppermute | solution.py:37
  66.1 9.2 %collective-permute-start.17 = (bf16[256,256]{1,0:T(8,128)(2,1)}, bf16[256,256]{1,0:T(8,128)(2,1)S(1)}, u32[]{:S(2)}, u32[]{:S(2)}) collective-permute-start(bf16[256,256]{1,0:T(8,128)(2,1)} %get-tuple-element.37), channel_id=1, source_target_pairs={{0,4},{1,5},{2,6},{3,7},{4,0},{5,1},{6,2},{7,3},{8,12},{9,13},{10,... | collective-permute-start | bytes 393224 | tf_op jit(solution)/shard_map/ppermute | solution.py:37
  68.9 8.0 %collective-permute-start.16 = (bf16[256,256]{1,0:T(8,128)(2,1)}, bf16[256,256]{1,0:T(8,128)(2,1)S(1)}, u32[]{:S(2)}, u32[]{:S(2)}) collective-permute-start(bf16[256,256]{1,0:T(8,128)(2,1)} %get-tuple-element.36), channel_id=1, source_target_pairs={{0,5},{1,4},{2,7},{3,6},{4,1},{5,0},{6,3},{7,2},{8,13},{9,12},{10,... | collective-permute-start | bytes 393224 | tf_op jit(solution)/shard_map/ppermute | solution.py:37
  79.5 10.7 %collective-permute-start.27 = (bf16[2,256,128]{2,1,0:T(8,128)(2,1)S(1)}, bf16[2,256,128]{2,1,0:T(8,128)(2,1)S(1)}, u32[]{:S(2)}, u32[]{:S(2)}) collective-permute-start(bf16[2,256,128]{2,1,0:T(8,128)(2,1)S(1)} %bitcast.36), channel_id=1, source_target_pairs={{0,4},{1,5},{2,6},{3,7},{4,0},{5,1},{6,2},{7,3},{8,12},{9,13},{10,... | collective-permute-start | bytes 393224 | tf_op jit(solution)/shard_map/ppermute | solution.py:37
  83.2 9.3 %collective-permute-start.29 = (bf16[2,256,128]{2,1,0:T(8,128)(2,1)S(1)}, bf16[2,256,128]{2,1,0:T(8,128)(2,1)S(1)}, u32[]{:S(2)}, u32[]{:S(2)}) collective-permute-start(bf16[2,256,128]{2,1,0:T(8,128)(2,1)S(1)} %bitcast.37), channel_id=1, source_target_pairs={{0,2},{1,3},{2,4},{3,5},{4,6},{5,7},{6,0},{7,1},{8,10},{9,11},{10,... | collective-permute-start | bytes 393224 | tf_op jit(solution)/shard_map/ppermute | solution.py:37
  85.9 9.3 %collective-permute-start.30 = (bf16[2,256,128]{2,1,0:T(8,128)(2,1)S(1)}, bf16[2,256,128]{2,1,0:T(8,128)(2,1)S(1)}, u32[]{:S(2)}, u32[]{:S(2)}) collective-permute-start(bf16[2,256,128]{2,1,0:T(8,128)(2,1)S(1)} %collective-permute-done.24), channel_id=1, source_target_pairs={{0,2},{1,3},{2,4},{3,5},{4,6},{5,7},{6,0},{7,1},{8,10},{9,11},{10,... | collective-permute-start | bytes 393224 | tf_op jit(solution)/shard_map/ppermute | solution.py:37
  103.1 9.3 %collective-permute-start.31 = (bf16[16,256,256]{2,1,0:T(8,128)(2,1)}, bf16[16,256,256]{2,1,0:T(8,128)(2,1)}, u32[]{:S(2)}, u32[]{:S(2)}) collective-permute-start(bf16[16,256,256]{2,1,0:T(8,128)(2,1)} %shard_map.132), channel_id=1, source_target_pairs={{0,8},{8,0},{16,24},{24,16},{32,40},{40,32},{48,56},{56,48},{64,72... | collective-permute-start | bytes 6291464 | tf_op jit(solution)/shard_map/ppermute | solution.py:33
  113.9 8.4 %collective-permute-start.33 = (bf16[2,256,256]{2,1,0:T(8,128)(2,1)S(1)}, bf16[2,256,256]{2,1,0:T(8,128)(2,1)S(1)}, u32[]{:S(2)}, u32[]{:S(2)}) collective-permute-start(bf16[2,256,256]{2,1,0:T(8,128)(2,1)S(1)} %get-tuple-element.46), channel_id=1, source_target_pairs={{0,112},{8,120},{16,0},{24,8},{32,16},{40,24},{48,32},{56,40},{64,... | collective-permute-start | bytes 786440 | tf_op jit(solution)/shard_map/ppermute | solution.py:33
  116.5 8.8 %collective-permute-start.32 = (bf16[2,256,256]{2,1,0:T(8,128)(2,1)S(1)}, bf16[2,256,256]{2,1,0:T(8,128)(2,1)S(1)}, u32[]{:S(2)}, u32[]{:S(2)}) collective-permute-start(bf16[2,256,256]{2,1,0:T(8,128)(2,1)S(1)} %get-tuple-element.45), channel_id=1, source_target_pairs={{0,16},{8,24},{16,32},{24,40},{32,48},{40,56},{48,64},{56,72},{64,... | collective-permute-start | bytes 786440 | tf_op jit(solution)/shard_map/ppermute | solution.py:33
  127.1 7.9 %collective-permute-start.34 = (bf16[2,256,256]{2,1,0:T(8,128)(2,1)S(1)}, bf16[2,256,256]{2,1,0:T(8,128)(2,1)S(1)}, u32[]{:S(2)}, u32[]{:S(2)}) collective-permute-start(bf16[2,256,256]{2,1,0:T(8,128)(2,1)S(1)} %get-tuple-element.47), channel_id=1, source_target_pairs={{0,16},{8,24},{16,32},{24,40},{32,48},{40,56},{48,64},{56,72},{64,... | collective-permute-start | bytes 786440 | tf_op jit(solution)/shard_map/ppermute | solution.py:33
  136.3 7.1 %collective-permute-start.36 = (bf16[2,256,256]{2,1,0:T(8,128)(2,1)S(1)}, bf16[2,256,256]{2,1,0:T(8,128)(2,1)S(1)}, u32[]{:S(2)}, u32[]{:S(2)}) collective-permute-start(bf16[2,256,256]{2,1,0:T(8,128)(2,1)S(1)} %get-tuple-element.49), channel_id=1, source_target_pairs={{0,16},{8,24},{16,32},{24,40},{32,48},{40,56},{48,64},{56,72},{64,... | collective-permute-start | bytes 786440 | tf_op jit(solution)/shard_map/ppermute | solution.py:33
  136.4 8.0 %collective-permute-start.37 = (bf16[2,256,256]{2,1,0:T(8,128)(2,1)S(1)}, bf16[2,256,256]{2,1,0:T(8,128)(2,1)S(1)}, u32[]{:S(2)}, u32[]{:S(2)}) collective-permute-start(bf16[2,256,256]{2,1,0:T(8,128)(2,1)S(1)} %get-tuple-element.50), channel_id=1, source_target_pairs={{0,112},{8,120},{16,0},{24,8},{32,16},{40,24},{48,32},{56,40},{64,... | collective-permute-start | bytes 786440 | tf_op jit(solution)/shard_map/ppermute | solution.py:33
  144.5 7.7 %collective-permute-start.23 = (bf16[602,256]{1,0:T(8,128)(2,1)}, bf16[602,256]{1,0:T(8,128)(2,1)}, u32[]{:S(2)}, u32[]{:S(2)}) collective-permute-start(bf16[602,256]{1,0:T(8,128)(2,1)} %bitcast.4), channel_id=1, source_target_pairs={{0,128},{8,136},{16,144},{24,152},{32,160},{40,168},{48,176},{56,1... | collective-permute-start | bytes 924680 | tf_op jit(solution)/shard_map/ppermute | solution.py:33
  159.9 12.9 %all-to-all-start = ((f32[8,40,256]{2,1,0:T(8,128)}), f32[8,40,256]{2,1,0:T(8,128)S(1)}, u32[]{:S(2)}, u32[]{:S(2)}) async-start(f32[8,40,256]{2,1,0:T(8,128)} %bitcast.9), calls=%async_computation | async-start | bytes 655360 | tf_op jit(solution)/shard_map/all_to_all | solution.py:168
  (40 other events, 305.2 us)
where the time goes:
time: 206 us; the launch traced here: 205 us
  starting transfers between devices  69.5 us (34%)
  waiting for transfers between devices  58.1 us (28%)
  Pallas kernels  28.9 us (14%)
  blocking collectives  25.4 us (12%)
  other arithmetic  12.6 us (6%)
  local copies, waits for them, and re-layouts  5.62 us (3%)
  matrix products  3.66 us (2%)
    ppermute x28, starting transfers between devices, to_row(): return lax.ppermute(value, 'row', route)  44.9 us
    ppermute x28, waiting for transfers between devices, to_row(): return lax.ppermute(value, 'row', route)  33.7 us
    ppermute x14, starting transfers between devices, to_col(): return lax.ppermute(value, 'col', route)  20.7 us
    ppermute x14, waiting for transfers between devices, to_col(): return lax.ppermute(value, 'col', route)  16.4 us
    pallas_call x2, Pallas kernels, forward_part(): pl.pallas_call(functools.partial(forward_kernel, base, half, total is Non...  15.2 us
    all_to_all x1, blocking collectives, sum_everywhere(): every = lax.all_to_all(every, 'row', 0, 0, axis_index_groups=groups)  13.8 us
    pallas_call x2, Pallas kernels, backward_part(): pl.pallas_call(functools.partial(backward_kernel, base), in_specs=[smem]...  13.7 us
    all_to_all x1, blocking collectives, sum_everywhere(): lax.all_to_all(jnp.broadcast_to(part[None], (COLS,) + part.shape), 'col',...  11.5 us
  transfers between devices with their start and end apart: 43, of which 21 were waited for; matrix products, arithmetic and copies ran while one was open for 5% of the time, Pallas kernels for 8%

commit v1 on v0

--- a/solution.py
+++ b/solution.py
@@ -63,29 +63,32 @@
         carried = pltpu.make_async_copy(refs[half], total, total_sem)
         carried.start()
 
-    def step(q, _):
-        if not last:
-            pltpu.make_async_copy(pairs[0], held.at[q], held_sems.at[q]).wait()
-        for k in (2 * q, 2 * q + 1):
-            pltpu.make_async_copy(adj.at[0], tiles.at[k], tile_sems.at[k]).wait()
+    def step(p, _):
+        qs = [2 * p + i for i in range(2)]
         products = []
-        for far in range(2):
-            k = 2 * q + far
-            lhs = masked_tiles(tiles.at[k], cols, blocks[base + k] * slots)
-            products.append(jnp.dot(lhs, pairs[q][far] if last else held[q, far], preferred_element_type=F32))
-        if last and q == 0:
+        for q in qs:
+            if not last:
+                pltpu.make_async_copy(pairs[0], held.at[q], held_sems.at[q]).wait()
+            for k in (2 * q, 2 * q + 1):
+                pltpu.make_async_copy(adj.at[0], tiles.at[k], tile_sems.at[k]).wait()
+        for q in qs:
+            for far in range(2):
+                k = 2 * q + far
+                lhs = masked_tiles(tiles.at[k], cols, blocks[base + k] * slots)
+                rhs = pairs[q][far] if last else held[q, far]
+                products.append((k, jnp.dot(lhs, rhs, preferred_element_type=F32)))
+        if last:
             carried.wait()
-        for far in range(2):
-            first = blocks[base + 2 * q + far] * slots
+        for k, product in products:
+            first = blocks[base + k] * slots
             for s in range(slots):
-                total[rows[first + s]] += products[far][s * 128 : (s + 1) * 128]
+                total[rows[first + s]] += product[s * 128 : (s + 1) * 128]
         return 0
 
     if last:
-        for q in range(half):
-            step(q, 0)
+        step(0, 0)
     else:
-        lax.fori_loop(0, half, step, 0)
+        lax.fori_loop(0, half // 2, step, 0)
         carried = pltpu.make_async_copy(total, outs[0], total_sem)
         carried.start()
         carried.wait()
@@ -125,39 +128,58 @@
     return outs if last else outs[0]
 
 
-def backward_kernel(base, blocks, rows, cols, adj, grads, out, tiles, sems):
+def backward_kernel(base, blocks, rows, cols, adj, *refs):
+    pieces, (out, held, tiles, results, held_sems, tile_sems, out_sems) = refs[:COLS], refs[COLS:]
     count, slots = tiles.shape[:2]
+    arrivals = [
+        pltpu.make_async_copy(pieces[p], held.at[pl.ds(2 * p, 2)], held_sems.at[p]) for p in range(COLS)
+    ]
+    for arrival in arrivals:
+        arrival.start()
     for k in range(count):
-        pltpu.make_async_copy(adj.at[blocks[base + k]], tiles.at[k], sems.at[k]).start()
+        pltpu.make_async_copy(adj.at[blocks[base + k]], tiles.at[k], tile_sems.at[k]).start()
+    for arrival in arrivals:
+        arrival.wait()
 
     def step(q, _):
-        for k in (2 * q, 2 * q + 1):
-            pltpu.make_async_copy(adj.at[0], tiles.at[k], sems.at[k]).wait()
-        for k in (2 * q, 2 * q + 1):
+        ks = [8 * q + i for i in range(8)]
+        for k in ks:
+            pltpu.make_async_copy(adj.at[0], tiles.at[k], tile_sems.at[k]).wait()
+        for k in ks:
             first = blocks[base + k] * slots
             rhs = masked_tiles(tiles.at[k], cols, first)
-            lhs = jnp.concatenate([grads[rows[first + s]] for s in range(slots)], axis=1)
-            product = jnp.dot(lhs, rhs, preferred_element_type=F32)
-            out[k] = product.astype(BF)
+            lhs = jnp.concatenate([held[rows[first + s]] for s in range(slots)], axis=1)
+            results[k] = jnp.dot(lhs, rhs, preferred_element_type=F32).astype(BF)
+        for k in ks:
+            pltpu.make_async_copy(results.at[k], out.at[k], out_sems.at[k]).start()
         return 0
 
-    lax.fori_loop(0, count // 2, step, 0)
+    lax.fori_loop(0, count // 8, step, 0)
+    for k in range(count):
+        pltpu.make_async_copy(results.at[k], out.at[k], out_sems.at[k]).wait()
 
 
 def backward_part(adj, rows, cols, blocks, base, count, grads):
     slots = adj.shape[1]
-    smem, vmem = pl.BlockSpec(memory_space=pltpu.SMEM), pl.BlockSpec(memory_space=pltpu.VMEM)
+    smem, hbm = pl.BlockSpec(memory_space=pltpu.SMEM), pl.BlockSpec(memory_space=pltpu.HBM)
     return pl.pallas_call(
         functools.partial(backward_kernel, base),
-        in_specs=[smem] * 3 + [pl.BlockSpec(memory_space=pltpu.HBM)] + [vmem],
-        out_specs=vmem,
+        in_specs=[smem] * 3 + [hbm] * (1 + COLS),
+        out_specs=hbm,
         out_shape=jax.ShapeDtypeStruct((count, 256, 256), BF),
-        scratch_shapes=[pltpu.VMEM((count, slots, 128, 128), BF), pltpu.SemaphoreType.DMA((count,))],
+        scratch_shapes=[
+            pltpu.VMEM((16, 256, 128), BF),
+            pltpu.VMEM((count, slots, 128, 128), BF),
+            pltpu.VMEM((count, 256, 256), BF),
+            pltpu.SemaphoreType.DMA((COLS,)),
+            pltpu.SemaphoreType.DMA((count,)),
+            pltpu.SemaphoreType.DMA((count,)),
+        ],
         cost_estimate=pl.CostEstimate(
             flops=2 * count * 768 * 256 * 256, bytes_accessed=count * (1 << 19) + (1 << 20), transcendentals=0
         ),
         compiler_params=pltpu.CompilerParams(vmem_limit_bytes=VMEM),
-    )(blocks, rows, cols, adj, grads)
+    )(blocks, rows, cols, adj, *grads)
 
 
 def sum_everywhere(value, core, beside):
@@ -228,7 +250,7 @@
         pieces[2 * d] = to_col(mine, ring_y(-d))
     for d in (1, 3, 2):
         pieces[2 * d + 1] = to_col(across_x, ring_y(-d))
-    grads = jnp.concatenate(pieces, axis=0)
+    grads = pieces
 
     theirs = backward_part(adj, near, cols, blocks, 32, 16, grads)
     theirs, grads = lax.optimization_barrier((theirs, grads))
@@ -246,12 +268,17 @@
     up, down = to_row(up, ring_z(1)), to_row(down, ring_z(-1))
     features_t = features.T
     for k in (3, 2, 1):
-        up, down = add(k, up).astype(BF), (add(1 - k, down).astype(BF) if k > 1 else down)
-        up, down = lax.optimization_barrier((up, down))
-        up, down = to_row(up, ring_z(1)), (to_row(down, ring_z(-1)) if k > 1 else down)
+        here_up, here_down = add(k), (add(1 - k) if k > 1 else add(0))
+        up, down, here_up, here_down = lax.optimization_barrier((up, down, here_up, here_down))
+        up = (here_up + up.astype(F32)).astype(BF)
+        if k > 1:
+            down = (here_down + down.astype(F32)).astype(BF)
+            up, down = lax.optimization_barrier((up, down))
+            down = to_row(down, ring_z(-1))
+        up = to_row(up, ring_z(1))
         if k == 2:
             features_x = to_row(features_t, XLO)
-    both = add(0, up, down)
+    both = here_down + up.astype(F32) + down.astype(F32)
     across_x = both[1].astype(BF)
 
     grad_scale = 1.0 / math.sqrt(ROWS * COLS * features.shape[0])

time: 206 us -> 196 us (0.951)
  waiting for transfers between devices: 58.1 us -> 51.7 us
  starting transfers between devices: 69.5 us -> 75.5 us
  other arithmetic: 12.6 us -> 8.77 us
  Pallas kernels: 28.9 us -> 26.3 us
    convert_element_type x4 -> x5, other arithmetic: 5.1 us -> 0.31 us  [the longest x3 0.19 us: body(): up = (here_up + up.astype(F32)).astype(BF)]
    ppermute x14, starting transfers between devices: 20.7 us -> 24.6 us  [to_col(): return lax.ppermute(value, 'col', route)]
    ppermute x14, waiting for transfers between devices: 16.4 us -> 12.9 us  [to_col(): return lax.ppermute(value, 'col', route)]
    ppermute x28, waiting for transfers between devices: 33.7 us -> 30.9 us  [to_row(): return lax.ppermute(value, 'row', route)]
    ppermute x28, starting transfers between devices: 44.9 us -> 47 us  [to_row(): return lax.ppermute(value, 'row', route)]
    unnamed x51 -> x58, local copies, waits for them, and re-layouts: 5.1 us -> 4.65 us
  transfers between devices with their start and end apart: 43 -> 43, of which waited for: 21 -> 22; matrix products, arithmetic and copies ran while one was open for 5% -> 4% of each run, Pallas kernels for 8% -> 8%
where the time goes in v1:
time: 196 us
  starting transfers between devices  75.5 us (39%)
  waiting for transfers between devices  51.7 us (26%)
  Pallas kernels  26.3 us (13%)
  blocking collectives  24.5 us (12%)
  other arithmetic  8.77 us (4%)
  local copies, waits for them, and re-layouts  5.16 us (3%)
  matrix products  2.6 us (1%)
    ppermute x28, starting transfers between devices, to_row(): return lax.ppermute(value, 'row', route)  47 us
    ppermute x28, waiting for transfers between devices, to_row(): return lax.ppermute(value, 'row', route)  30.9 us
    ppermute x14, starting transfers between devices, to_col(): return lax.ppermute(value, 'col', route)  24.6 us
    pallas_call x2, Pallas kernels, forward_part(): pl.pallas_call(functools.partial(forward_kernel, base, half, total is Non...  13.9 us
    all_to_all x1, blocking collectives, sum_everywhere(): every = lax.all_to_all(every, 'row', 0, 0, axis_index_groups=groups)  13.1 us
    ppermute x14, waiting for transfers between devices, to_col(): return lax.ppermute(value, 'col', route)  12.9 us
    pallas_call x2, Pallas kernels, backward_part(): pl.pallas_call(functools.partial(backward_kernel, base), in_specs=[smem]...  12.4 us
    all_to_all x1, blocking collectives, sum_everywhere(): lax.all_to_all(jnp.broadcast_to(part[None], (COLS,) + part.shape), 'col',...  11.5 us
  transfers between devices with their start and end apart: 43, of which 22 were waited for; matrix products, arithmetic and copies ran while one was open for 4% of the time, Pallas kernels for 8%

profile of v1, /device:TPU:1, one launch (start us, length us, event | category | flops | bytes accessed | tf_op | source)
XLA Modules:
  0.0 195.8 jit_solution(9400335022015797857)
XLA Ops:
  9.9 4.0 %collective-permute-start.7 = (bf16[2,256,256]{2,1,0:T(8,128)(2,1)S(1)}, bf16[2,256,256]{2,1,0:T(8,128)(2,1)S(1)}, u32[]{:S(2)}, u32[]{:S(2)}) collective-permute-start(bf16[2,256,256]{2,1,0:T(8,128)(2,1)S(1)} %pad_maximum_fusion.1.refs_0_), channel_id=1, source_target_pairs={{0,112},{8,120},{16,0},{24,8},{32,16},{40,24},{48,32},{56,40},{64,... | collective-permute-start | bytes 786440 | tf_op jit(solution)/shard_map/ppermute | solution.py:33
  21.6 2.7 %collective-permute-start.5 = (bf16[2,256,256]{2,1,0:T(8,128)(2,1)S(1)}, bf16[2,256,256]{2,1,0:T(8,128)(2,1)S(1)}, u32[]{:S(2)}, u32[]{:S(2)}) collective-permute-start(bf16[2,256,256]{2,1,0:T(8,128)(2,1)S(1)} %pad_maximum_fusion.1.refs_0_), channel_id=1, source_target_pairs={{0,8},{8,0},{16,24},{24,16},{32,40},{40,32},{48,56},{56,48},{64,72... | collective-permute-start | bytes 786440 | tf_op jit(solution)/shard_map/ppermute | solution.py:33
  28.4 3.7 %collective-permute-start.8 = (bf16[2,256,256]{2,1,0:T(8,128)(2,1)S(1)}, bf16[2,256,256]{2,1,0:T(8,128)(2,1)S(1)}, u32[]{:S(2)}, u32[]{:S(2)}) collective-permute-start(bf16[2,256,256]{2,1,0:T(8,128)(2,1)S(1)} %collective-permute-done.7.refs_4_), channel_id=1, source_target_pairs={{0,8},{8,0},{16,24},{24,16},{32,40},{40,32},{48,56},{56,48},{64,72... | collective-permute-start | bytes 786440 | tf_op jit(solution)/shard_map/ppermute | solution.py:33
  32.6 3.8 %collective-permute-start.12 = (bf16[2,256,256]{2,1,0:T(8,128)(2,1)S(1)}, bf16[2,256,256]{2,1,0:T(8,128)(2,1)S(1)}, u32[]{:S(2)}, u32[]{:S(2)}) collective-permute-start(bf16[2,256,256]{2,1,0:T(8,128)(2,1)S(1)} %collective-permute-done.3.refs_10_), channel_id=1, source_target_pairs={{0,8},{8,0},{16,24},{24,16},{32,40},{40,32},{48,56},{56,48},{64,72... | collective-permute-start | bytes 786440 | tf_op jit(solution)/shard_map/ppermute | solution.py:33
  38.8 9.5 %shard_map.130.refs_2_ = f32[16,128,256]{2,1,0:T(8,128)} custom-call(s32[64]{0:T(128)} %fusion.16.blocks, s32[192]{0:T(256)} %get-tuple-element.47.rows, s32[192]{0:T(256)} %get-tuple-element.48.cols, bf16[32,6,128,128]{3,2,1,0:T(8,128)(2,1)} %bitcast.27, bf16[2,256,256]{2,1,0:T(8,128)(2,1)} %copy-done.2, bf16[2,256,256]{2,1,0:T(8,128)(2,1)} %copy-done.14, ...), custom_call_target="tpu_custom_call" | custom-call | flops 2818572288 | bytes 18874368 | tf_op jit(solution)/shard_map/pallas_call | solution.py:110
  50.9 4.4 %shard_map.131 = (f32[256,256]{1,0:T(8,128)}, bf16[256,256]{1,0:T(8,128)(2,1)}, bf16[256,256]{1,0:T(8,128)(2,1)}, bf16[256,256]{1,0:T(8,128)(2,1)}, bf16[256,256...) custom-call(s32[64]{0:T(128)} %fusion.16.blocks, ...), custom_call_target="tpu_custom_call" | custom-call | flops 402653184 | bytes 6291456 | tf_op jit(solution)/shard_map/pallas_call | solution.py:110
  55.3 5.5 %collective-permute-start.16 = (bf16[256,256]{1,0:T(8,128)(2,1)}, bf16[256,256]{1,0:T(8,128)(2,1)S(1)}, u32[]{:S(2)}, u32[]{:S(2)}) collective-permute-start(bf16[256,256]{1,0:T(8,128)(2,1)} %get-tuple-element.53), channel_id=1, source_target_pairs={{0,5},{1,4},{2,7},{3,6},{4,1},{5,0},{6,3},{7,2},{8,13},{9,12},{10,... | collective-permute-start | bytes 393224 | tf_op jit(solution)/shard_map/ppermute | solution.py:37
  63.4 3.8 %collective-permute-start.20 = (bf16[256,256]{1,0:T(8,128)(2,1)}, bf16[256,256]{1,0:T(8,128)(2,1)S(1)}, u32[]{:S(2)}, u32[]{:S(2)}) collective-permute-start(bf16[256,256]{1,0:T(8,128)(2,1)} %get-tuple-element.57), channel_id=1, source_target_pairs={{0,7},{1,6},{2,1},{3,0},{4,3},{5,2},{6,5},{7,4},{8,15},{9,14},{10,... | collective-permute-start | bytes 393224 | tf_op jit(solution)/shard_map/ppermute | solution.py:37
  67.4 2.7 %collective-permute-done.17 = bf16[256,256]{1,0:T(8,128)(2,1)S(1)} collective-permute-done((bf16[256,256]{1,0:T(8,128)(2,1)}, bf16[256,256]{1,0:T(8,128)(2,1)S(1)}, u32[]{:S(2)}, u32[]{:S(2)}) %collective-permute-start.17) | collective-permute-done | bytes 131104 | tf_op jit(solution)/shard_map/ppermute | solution.py:37
  70.1 3.2 %collective-permute-start.22 = (bf16[256,256]{1,0:T(8,128)(2,1)}, bf16[256,256]{1,0:T(8,128)(2,1)S(1)}, u32[]{:S(2)}, u32[]{:S(2)}) collective-permute-start(bf16[256,256]{1,0:T(8,128)(2,1)} %get-tuple-element.59), channel_id=1, source_target_pairs={{0,1},{1,0},{2,3},{3,2},{4,5},{5,4},{6,7},{7,6},{8,9},{9,8},{10,11... | collective-permute-start | bytes 393224 | tf_op jit(solution)/shard_map/ppermute | solution.py:37
  77.2 3.7 %collective-permute-start.24 = (bf16[2,256,128]{2,1,0:T(8,128)(2,1)S(1)}, bf16[2,256,128]{2,1,0:T(8,128)(2,1)S(1)}, u32[]{:S(2)}, u32[]{:S(2)}) collective-permute-start(bf16[2,256,128]{2,1,0:T(8,128)(2,1)S(1)} %bitcast.32), channel_id=1, source_target_pairs={{0,1},{1,0},{2,3},{3,2},{4,5},{5,4},{6,7},{7,6},{8,9},{9,8},{10,11... | collective-permute-start | bytes 393224 | tf_op jit(solution)/shard_map/ppermute | solution.py:37
  94.9 6.2 %shard_map.132 = bf16[16,256,256]{2,1,0:T(8,128)(2,1)} custom-call(s32[64]{0:T(128)} %fusion.16.blocks, s32[192]{0:T(256)} %get-tuple-element.47.rows, s32[192]{0:T(256)} %get-tuple-element.48.cols, bf16[32,6,128,128]{3,2,1,0:T(8,128)(2,1)} %bitcast.29, bf16[2,256,128]{2,1,0:T(8,128)(2,1)} %bitcast.36, bf16[2,256,128]{2,1,0:T(8,128)(2,1)} %copy-done.3, ...), custom_call_target="tpu_custom_call" | custom-call | flops 1610612736 | bytes 9437184 | tf_op jit(solution)/shard_map/pallas_call | solution.py:165
  101.1 2.9 %collective-permute-start.31 = (bf16[16,256,256]{2,1,0:T(8,128)(2,1)}, bf16[16,256,256]{2,1,0:T(8,128)(2,1)S(1)}, u32[]{:S(2)}, u32[]{:S(2)}) collective-permute-start(bf16[16,256,256]{2,1,0:T(8,128)(2,1)} %shard_map.132), channel_id=1, source_target_pairs={{0,8},{8,0},{16,24},{24,16},{32,40},{40,32},{48,56},{56,48},{64,72... | collective-permute-start | bytes 6291464 | tf_op jit(solution)/shard_map/ppermute | solution.py:33
  104.0 6.2 %shard_map.133 = bf16[16,256,256]{2,1,0:T(8,128)(2,1)} custom-call(s32[64]{0:T(128)} %fusion.16.blocks, s32[192]{0:T(256)} %get-tuple-element.47.rows, s32[192]{0:T(256)} %get-tuple-element.48.cols, bf16[32,6,128,128]{3,2,1,0:T(8,128)(2,1)} %bitcast.30, bf16[2,256,128]{2,1,0:T(8,128)(2,1)} %bitcast.37, bf16[2,256,128]{2,1,0:T(8,128)(2,1)} %copy-done.3, ...), custom_call_target="tpu_custom_call" | custom-call | flops 1610612736 | bytes 9437184 | tf_op jit(solution)/shard_map/pallas_call | solution.py:165
  115.0 6.5 %collective-permute-done.32 = bf16[2,256,256]{2,1,0:T(8,128)(2,1)S(1)} collective-permute-done((bf16[2,256,256]{2,1,0:T(8,128)(2,1)S(1)}, bf16[2,256,256]{2,1,0:T(8,128)(2,1)S(1)}, u32[]{:S(2)}, u32[]{:S(2)}) %collective-permute-start.32) | collective-permute-done | bytes 262176 | tf_op jit(solution)/shard_map/ppermute | solution.py:33
  125.3 5.6 %collective-permute-done.34 = bf16[2,256,256]{2,1,0:T(8,128)(2,1)S(1)} collective-permute-done((bf16[2,256,256]{2,1,0:T(8,128)(2,1)S(1)}, bf16[2,256,256]{2,1,0:T(8,128)(2,1)S(1)}, u32[]{:S(2)}, u32[]{:S(2)}) %collective-permute-start.34) | collective-permute-done | bytes 262176 | tf_op jit(solution)/shard_map/ppermute | solution.py:33
  133.7 4.6 %collective-permute-done.36 = bf16[2,256,256]{2,1,0:T(8,128)(2,1)S(1)} collective-permute-done((bf16[2,256,256]{2,1,0:T(8,128)(2,1)S(1)}, bf16[2,256,256]{2,1,0:T(8,128)(2,1)S(1)}, u32[]{:S(2)}, u32[]{:S(2)}) %collective-permute-start.36) | collective-permute-done | bytes 262176 | tf_op jit(solution)/shard_map/ppermute | solution.py:33
  139.5 5.4 %collective-permute-done.38 = bf16[2,256,256]{2,1,0:T(8,128)(2,1)S(1)} collective-permute-done((bf16[2,256,256]{2,1,0:T(8,128)(2,1)S(1)}, bf16[2,256,256]{2,1,0:T(8,128)(2,1)S(1)}, u32[]{:S(2)}, u32[]{:S(2)}) %collective-permute-start.38) | collective-permute-done | bytes 262176 | tf_op jit(solution)/shard_map/ppermute | solution.py:33
  145.5 4.1 %collective-permute-start.39 = (f32[320,256]{1,0:T(8,128)S(1)}, f32[320,256]{1,0:T(8,128)S(1)}, u32[]{:S(2)}, u32[]{:S(2)}) collective-permute-start(f32[320,256]{1,0:T(8,128)S(1)} %slice_select_fusion), channel_id=1, source_target_pairs={{0,8},{8,0},{16,24},{24,16},{32,40},{40,32},{48,56},{56,48},{64,72... | collective-permute-start | bytes 983048 | tf_op jit(solution)/shard_map/ppermute | solution.py:33
  151.6 3.9 %all-to-all-start = ((f32[8,40,256]{2,1,0:T(8,128)}), f32[8,40,256]{2,1,0:T(8,128)S(1)}, u32[]{:S(2)}, u32[]{:S(2)}) async-start(f32[8,40,256]{2,1,0:T(8,128)} %bitcast.9), calls=%async_computation | async-start | bytes 655360 | tf_op jit(solution)/shard_map/all_to_all | solution.py:190
  156.5 7.9 %all-to-all-done = f32[8,40,256]{2,1,0:T(8,128)S(1)} async-done(((f32[8,40,256]{2,1,0:T(8,128)}), f32[8,40,256]{2,1,0:T(8,128)S(1)}, u32[]{:S(2)}, u32[]{:S(2)}) %all-to-all-start) | async-done | bytes 327712 | tf_op jit(solution)/shard_map/all_to_all | solution.py:190
  164.5 13.1 %all_to_all.15 = bf16[16,40,256]{2,1,0:T(8,128)(2,1)S(1)} all-to-all(bf16[16,40,256]{2,1,0:T(8,128)(2,1)S(1)} %broadcast_in_dim.6), channel_id=1, replica_groups={{0,16,32,48,64,80,96,112,128,144,160,176,192,208,224,240},{8,24,40,56,7..., dimensions={0} | all-to-all | bytes 655360 | tf_op jit(solution)/shard_map/all_to_all | solution.py:194
  177.7 11.5 %all_to_all.16 = f32[8,40,256]{2,1,0:T(8,128)S(1)} all-to-all(f32[8,40,256]{2,1,0:T(8,128)S(1)} %broadcast_in_dim.7), channel_id=1, replica_groups=mesh['row'=32,'col'=8] {'col'}, dimensions={0} | all-to-all | bytes 655360 | tf_op jit(solution)/shard_map/all_to_all | solution.py:196
  189.2 4.4 %collective-permute-start.41 = (f32[320,256]{1,0:T(8,128)S(1)}, f32[320,256]{1,0:T(8,128)S(1)}, u32[]{:S(2)}, u32[]{:S(2)}) collective-permute-start(f32[320,256]{1,0:T(8,128)S(1)} %bitcast.31), channel_id=1, source_target_pairs={{0,8},{8,0},{16,24},{24,16},{32,40},{40,32},{48,56},{56,48},{64,72... | collective-permute-start | bytes 983048 | tf_op jit(solution)/shard_map/ppermute | solution.py:33
  (156 shorter events, 65.3 us)
Async XLA Ops:
  7.4 11.5 %collective-permute-start.1 = (bf16[2,256,256]{2,1,0:T(8,128)(2,1)S(1)}, bf16[2,256,256]{2,1,0:T(8,128)(2,1)S(1)}, u32[]{:S(2)}, u32[]{:S(2)}) collective-permute-start(bf16[2,256,256]{2,1,0:T(8,128)(2,1)S(1)} %pad_maximum_fusion.1.refs_0_), channel_id=1, source_target_pairs={{0,16},{8,24},{16,32},{24,40},{32,48},{40,56},{48,64},{56,72},{64,... | collective-permute-start | bytes 786440 | tf_op jit(solution)/shard_map/ppermute | solution.py:33
  9.9 9.0 %collective-permute-start.7 = (bf16[2,256,256]{2,1,0:T(8,128)(2,1)S(1)}, bf16[2,256,256]{2,1,0:T(8,128)(2,1)S(1)}, u32[]{:S(2)}, u32[]{:S(2)}) collective-permute-start(bf16[2,256,256]{2,1,0:T(8,128)(2,1)S(1)} %pad_maximum_fusion.1.refs_0_), channel_id=1, source_target_pairs={{0,112},{8,120},{16,0},{24,8},{32,16},{40,24},{48,32},{56,40},{64,... | collective-permute-start | bytes 786440 | tf_op jit(solution)/shard_map/ppermute | solution.py:33
  21.6 10.5 %collective-permute-start.5 = (bf16[2,256,256]{2,1,0:T(8,128)(2,1)S(1)}, bf16[2,256,256]{2,1,0:T(8,128)(2,1)S(1)}, u32[]{:S(2)}, u32[]{:S(2)}) collective-permute-start(bf16[2,256,256]{2,1,0:T(8,128)(2,1)S(1)} %pad_maximum_fusion.1.refs_0_), channel_id=1, source_target_pairs={{0,8},{8,0},{16,24},{24,16},{32,40},{40,32},{48,56},{56,48},{64,72... | collective-permute-start | bytes 786440 | tf_op jit(solution)/shard_map/ppermute | solution.py:33
  24.4 7.8 %collective-permute-start.6 = (bf16[2,256,256]{2,1,0:T(8,128)(2,1)S(1)}, bf16[2,256,256]{2,1,0:T(8,128)(2,1)S(1)}, u32[]{:S(2)}, u32[]{:S(2)}) collective-permute-start(bf16[2,256,256]{2,1,0:T(8,128)(2,1)S(1)} %collective-permute-done.1.refs_2_), channel_id=1, source_target_pairs={{0,8},{8,0},{16,24},{24,16},{32,40},{40,32},{48,56},{56,48},{64,72... | collective-permute-start | bytes 786440 | tf_op jit(solution)/shard_map/ppermute | solution.py:33
  25.8 10.7 %collective-permute-start.13 = (bf16[2,256,256]{2,1,0:T(8,128)(2,1)S(1)}, bf16[2,256,256]{2,1,0:T(8,128)(2,1)S(1)}, u32[]{:S(2)}, u32[]{:S(2)}) collective-permute-start(bf16[2,256,256]{2,1,0:T(8,128)(2,1)S(1)} %collective-permute-done.10.refs_8_), channel_id=1, source_target_pairs={{0,112},{8,120},{16,0},{24,8},{32,16},{40,24},{48,32},{56,40},{64,... | collective-permute-start | bytes 786440 | tf_op jit(solution)/shard_map/ppermute | solution.py:33
  28.4 8.1 %collective-permute-start.8 = (bf16[2,256,256]{2,1,0:T(8,128)(2,1)S(1)}, bf16[2,256,256]{2,1,0:T(8,128)(2,1)S(1)}, u32[]{:S(2)}, u32[]{:S(2)}) collective-permute-start(bf16[2,256,256]{2,1,0:T(8,128)(2,1)S(1)} %collective-permute-done.7.refs_4_), channel_id=1, source_target_pairs={{0,8},{8,0},{16,24},{24,16},{32,40},{40,32},{48,56},{56,48},{64,72... | collective-permute-start | bytes 786440 | tf_op jit(solution)/shard_map/ppermute | solution.py:33
  36.6 11.8 %collective-permute-start.4 = (bf16[2,256,256]{2,1,0:T(8,128)(2,1)S(1)}, bf16[2,256,256]{2,1,0:T(8,128)(2,1)S(1)}, u32[]{:S(2)}, u32[]{:S(2)}) collective-permute-start(bf16[2,256,256]{2,1,0:T(8,128)(2,1)S(1)} %collective-permute-done.3.refs_10_), channel_id=1, source_target_pairs={{0,16},{8,24},{16,32},{24,40},{32,48},{40,56},{48,64},{56,72},{64,... | collective-permute-start | bytes 786440 | tf_op jit(solution)/shard_map/ppermute | solution.py:33
  55.3 11.9 %collective-permute-start.16 = (bf16[256,256]{1,0:T(8,128)(2,1)}, bf16[256,256]{1,0:T(8,128)(2,1)S(1)}, u32[]{:S(2)}, u32[]{:S(2)}) collective-permute-start(bf16[256,256]{1,0:T(8,128)(2,1)} %get-tuple-element.53), channel_id=1, source_target_pairs={{0,5},{1,4},{2,7},{3,6},{4,1},{5,0},{6,3},{7,2},{8,13},{9,12},{10,... | collective-permute-start | bytes 393224 | tf_op jit(solution)/shard_map/ppermute | solution.py:37
  60.8 9.3 %collective-permute-start.17 = (bf16[256,256]{1,0:T(8,128)(2,1)}, bf16[256,256]{1,0:T(8,128)(2,1)S(1)}, u32[]{:S(2)}, u32[]{:S(2)}) collective-permute-start(bf16[256,256]{1,0:T(8,128)(2,1)} %get-tuple-element.54), channel_id=1, source_target_pairs={{0,4},{1,5},{2,6},{3,7},{4,0},{5,1},{6,2},{7,3},{8,12},{9,13},{10,... | collective-permute-start | bytes 393224 | tf_op jit(solution)/shard_map/ppermute | solution.py:37
  60.8 12.5 %collective-permute-start.18 = (bf16[256,256]{1,0:T(8,128)(2,1)}, bf16[256,256]{1,0:T(8,128)(2,1)S(1)}, u32[]{:S(2)}, u32[]{:S(2)}) collective-permute-start(bf16[256,256]{1,0:T(8,128)(2,1)} %get-tuple-element.55), channel_id=1, source_target_pairs={{0,3},{1,2},{2,5},{3,4},{4,7},{5,6},{6,1},{7,0},{8,11},{9,10},{10,... | collective-permute-start | bytes 393224 | tf_op jit(solution)/shard_map/ppermute | solution.py:37
  62.0 11.3 %collective-permute-start.19 = (bf16[256,256]{1,0:T(8,128)(2,1)}, bf16[256,256]{1,0:T(8,128)(2,1)S(1)}, u32[]{:S(2)}, u32[]{:S(2)}) collective-permute-start(bf16[256,256]{1,0:T(8,128)(2,1)} %get-tuple-element.56), channel_id=1, source_target_pairs={{0,2},{1,3},{2,4},{3,5},{4,6},{5,7},{6,0},{7,1},{8,10},{9,11},{10,... | collective-permute-start | bytes 393224 | tf_op jit(solution)/shard_map/ppermute | solution.py:37
  63.4 10.0 %collective-permute-start.20 = (bf16[256,256]{1,0:T(8,128)(2,1)}, bf16[256,256]{1,0:T(8,128)(2,1)S(1)}, u32[]{:S(2)}, u32[]{:S(2)}) collective-permute-start(bf16[256,256]{1,0:T(8,128)(2,1)} %get-tuple-element.57), channel_id=1, source_target_pairs={{0,7},{1,6},{2,1},{3,0},{4,3},{5,2},{6,5},{7,4},{8,15},{9,14},{10,... | collective-permute-start | bytes 393224 | tf_op jit(solution)/shard_map/ppermute | solution.py:37
  67.2 7.0 %collective-permute-start.21 = (bf16[256,256]{1,0:T(8,128)(2,1)}, bf16[256,256]{1,0:T(8,128)(2,1)S(1)}, u32[]{:S(2)}, u32[]{:S(2)}) collective-permute-start(bf16[256,256]{1,0:T(8,128)(2,1)} %get-tuple-element.58), channel_id=1, source_target_pairs={{0,6},{1,7},{2,0},{3,1},{4,2},{5,3},{6,4},{7,5},{8,14},{9,15},{10,... | collective-permute-start | bytes 393224 | tf_op jit(solution)/shard_map/ppermute | solution.py:37
  81.4 7.2 %collective-permute-start.29 = (bf16[2,256,128]{2,1,0:T(8,128)(2,1)S(1)}, bf16[2,256,128]{2,1,0:T(8,128)(2,1)S(1)}, u32[]{:S(2)}, u32[]{:S(2)}) collective-permute-start(bf16[2,256,128]{2,1,0:T(8,128)(2,1)S(1)} %bitcast.35), channel_id=1, source_target_pairs={{0,2},{1,3},{2,4},{3,5},{4,6},{5,7},{6,0},{7,1},{8,10},{9,11},{10,... | collective-permute-start | bytes 393224 | tf_op jit(solution)/shard_map/ppermute | solution.py:37
  84.9 7.5 %collective-permute-start.28 = (bf16[2,256,128]{2,1,0:T(8,128)(2,1)S(1)}, bf16[2,256,128]{2,1,0:T(8,128)(2,1)S(1)}, u32[]{:S(2)}, u32[]{:S(2)}) collective-permute-start(bf16[2,256,128]{2,1,0:T(8,128)(2,1)S(1)} %collective-permute-done.24.refs_1_), channel_id=1, source_target_pairs={{0,4},{1,5},{2,6},{3,7},{4,0},{5,1},{6,2},{7,3},{8,12},{9,13},{10,... | collective-permute-start | bytes 393224 | tf_op jit(solution)/shard_map/ppermute | solution.py:37
  86.5 7.6 %collective-permute-start.30 = (bf16[2,256,128]{2,1,0:T(8,128)(2,1)S(1)}, bf16[2,256,128]{2,1,0:T(8,128)(2,1)S(1)}, u32[]{:S(2)}, u32[]{:S(2)}) collective-permute-start(bf16[2,256,128]{2,1,0:T(8,128)(2,1)S(1)} %collective-permute-done.24.refs_1_), channel_id=1, source_target_pairs={{0,2},{1,3},{2,4},{3,5},{4,6},{5,7},{6,0},{7,1},{8,10},{9,11},{10,... | collective-permute-start | bytes 393224 | tf_op jit(solution)/shard_map/ppermute | solution.py:37
  101.1 9.1 %collective-permute-start.31 = (bf16[16,256,256]{2,1,0:T(8,128)(2,1)}, bf16[16,256,256]{2,1,0:T(8,128)(2,1)S(1)}, u32[]{:S(2)}, u32[]{:S(2)}) collective-permute-start(bf16[16,256,256]{2,1,0:T(8,128)(2,1)} %shard_map.132), channel_id=1, source_target_pairs={{0,8},{8,0},{16,24},{24,16},{32,40},{40,32},{48,56},{56,48},{64,72... | collective-permute-start | bytes 6291464 | tf_op jit(solution)/shard_map/ppermute | solution.py:33
  112.2 9.2 %collective-permute-start.32 = (bf16[2,256,256]{2,1,0:T(8,128)(2,1)S(1)}, bf16[2,256,256]{2,1,0:T(8,128)(2,1)S(1)}, u32[]{:S(2)}, u32[]{:S(2)}) collective-permute-start(bf16[2,256,256]{2,1,0:T(8,128)(2,1)S(1)} %get-tuple-element.69), channel_id=1, source_target_pairs={{0,16},{8,24},{16,32},{24,40},{32,48},{40,56},{48,64},{56,72},{64,... | collective-permute-start | bytes 786440 | tf_op jit(solution)/shard_map/ppermute | solution.py:33
  113.0 9.4 %collective-permute-start.33 = (bf16[2,256,256]{2,1,0:T(8,128)(2,1)S(1)}, bf16[2,256,256]{2,1,0:T(8,128)(2,1)S(1)}, u32[]{:S(2)}, u32[]{:S(2)}) collective-permute-start(bf16[2,256,256]{2,1,0:T(8,128)(2,1)S(1)} %get-tuple-element.70), channel_id=1, source_target_pairs={{0,112},{8,120},{16,0},{24,8},{32,16},{40,24},{48,32},{56,40},{64,... | collective-permute-start | bytes 786440 | tf_op jit(solution)/shard_map/ppermute | solution.py:33
  122.5 8.3 %collective-permute-start.34 = (bf16[2,256,256]{2,1,0:T(8,128)(2,1)S(1)}, bf16[2,256,256]{2,1,0:T(8,128)(2,1)S(1)}, u32[]{:S(2)}, u32[]{:S(2)}) collective-permute-start(bf16[2,256,256]{2,1,0:T(8,128)(2,1)S(1)} %add_convert_fusion.4), channel_id=1, source_target_pairs={{0,16},{8,24},{16,32},{24,40},{32,48},{40,56},{48,64},{56,72},{64,... | collective-permute-start | bytes 786440 | tf_op jit(solution)/shard_map/ppermute | solution.py:33
  123.7 7.1 %collective-permute-start.35 = (bf16[2,256,256]{2,1,0:T(8,128)(2,1)S(1)}, bf16[2,256,256]{2,1,0:T(8,128)(2,1)S(1)}, u32[]{:S(2)}, u32[]{:S(2)}) collective-permute-start(bf16[2,256,256]{2,1,0:T(8,128)(2,1)S(1)} %add_convert_fusion.3), channel_id=1, source_target_pairs={{0,112},{8,120},{16,0},{24,8},{32,16},{40,24},{48,32},{56,40},{64,... | collective-permute-start | bytes 786440 | tf_op jit(solution)/shard_map/ppermute | solution.py:33
  131.0 7.4 %collective-permute-start.36 = (bf16[2,256,256]{2,1,0:T(8,128)(2,1)S(1)}, bf16[2,256,256]{2,1,0:T(8,128)(2,1)S(1)}, u32[]{:S(2)}, u32[]{:S(2)}) collective-permute-start(bf16[2,256,256]{2,1,0:T(8,128)(2,1)S(1)} %add_convert_fusion.2), channel_id=1, source_target_pairs={{0,16},{8,24},{16,32},{24,40},{32,48},{40,56},{48,64},{56,72},{64,... | collective-permute-start | bytes 786440 | tf_op jit(solution)/shard_map/ppermute | solution.py:33
  131.3 7.0 %collective-permute-start.37 = (bf16[2,256,256]{2,1,0:T(8,128)(2,1)S(1)}, bf16[2,256,256]{2,1,0:T(8,128)(2,1)S(1)}, u32[]{:S(2)}, u32[]{:S(2)}) collective-permute-start(bf16[2,256,256]{2,1,0:T(8,128)(2,1)S(1)} %add_convert_fusion.1), channel_id=1, source_target_pairs={{0,112},{8,120},{16,0},{24,8},{32,16},{40,24},{48,32},{56,40},{64,... | collective-permute-start | bytes 786440 | tf_op jit(solution)/shard_map/ppermute | solution.py:33
  151.6 12.9 %all-to-all-start = ((f32[8,40,256]{2,1,0:T(8,128)}), f32[8,40,256]{2,1,0:T(8,128)S(1)}, u32[]{:S(2)}, u32[]{:S(2)}) async-start(f32[8,40,256]{2,1,0:T(8,128)} %bitcast.9), calls=%async_computation | async-start | bytes 655360 | tf_op jit(solution)/shard_map/all_to_all | solution.py:190
  (47 other events, 356.4 us)

commit v2 on v1

--- a/solution.py
+++ b/solution.py
@@ -131,6 +131,7 @@
 def backward_kernel(base, blocks, rows, cols, adj, *refs):
     pieces, (out, held, tiles, results, held_sems, tile_sems, out_sems) = refs[:COLS], refs[COLS:]
     count, slots = tiles.shape[:2]
+    group = 8 if count % 8 == 0 else 4
     arrivals = [
         pltpu.make_async_copy(pieces[p], held.at[pl.ds(2 * p, 2)], held_sems.at[p]) for p in range(COLS)
     ]
@@ -142,7 +143,7 @@
         arrival.wait()
 
     def step(q, _):
-        ks = [8 * q + i for i in range(8)]
+        ks = [group * q + i for i in range(group)]
         for k in ks:
             pltpu.make_async_copy(adj.at[0], tiles.at[k], tile_sems.at[k]).wait()
         for k in ks:
@@ -154,7 +155,7 @@
             pltpu.make_async_copy(results.at[k], out.at[k], out_sems.at[k]).start()
         return 0
 
-    lax.fori_loop(0, count // 8, step, 0)
+    lax.fori_loop(0, count // group, step, 0)
     for k in range(count):
         pltpu.make_async_copy(results.at[k], out.at[k], out_sems.at[k]).wait()
 
@@ -187,7 +188,8 @@
     mine = jnp.where(core == 0, halves[0], halves[1])
     other = jnp.where(core == 0, halves[1], halves[0])
     part = mine + to_row(other, CORE)
-    part = jnp.sum(lax.all_to_all(part.reshape(COLS, 40, 256), "col", 0, 0), axis=0)
+    parts = lax.all_to_all(part.astype(BF).reshape(COLS, 40, 256), "col", 0, 0)
+    part = jnp.sum(parts.astype(F32), axis=0)
     part, beside = lax.optimization_barrier((part, beside))
     groups = [[2 * i + c for i in range(ROWS // 2)] for c in range(2)]
     every = jnp.broadcast_to(part.astype(BF)[None], (ROWS // 2,) + part.shape)
@@ -234,7 +236,7 @@
     parts = forward_part(adj, near, cols, blocks, 28, [up, to_row(up, CORE)], total, True)
 
     pre_act = parts[0]
-    for d, far in ((2, 1), (2, 0), (1, 1), (1, 0), (3, 1), (3, 0), (0, 1)):
+    for d, far in ((0, 1), (1, 0), (3, 0), (2, 0), (1, 1), (3, 1), (2, 1)):
         route = [(i, (i + 2 * d) % COLS ^ far) for i in range(COLS)]
         pre_act = pre_act + to_col(parts[2 * d + far], route).astype(F32)
     gate = jax.nn.sigmoid(pre_act)
@@ -255,17 +257,17 @@
     theirs = backward_part(adj, near, cols, blocks, 32, 16, grads)
     theirs, grads = lax.optimization_barrier((theirs, grads))
     theirs = to_row(theirs, CORE)
-    ours = backward_part(adj, near, cols, blocks, 48, 16, grads)
-
-    def add(d, *arrived):
+    first = backward_part(adj, near, cols, blocks, 48, 4, grads)
+
+    sums = (first.astype(F32) + theirs[:4].astype(F32)).astype(BF)
+    up, down, grads = lax.optimization_barrier((sums[:2], sums[2:], grads))
+    up, down = to_row(up, ring_z(1)), to_row(down, ring_z(-1))
+    rest = backward_part(adj, near, cols, blocks, 52, 12, grads)
+
+    def add(d):
         k = 2 * FAR_FIRST.index(d)
-        total = ours[k : k + 2].astype(F32) + theirs[k : k + 2].astype(F32)
-        for value in arrived:
-            total = total + value.astype(F32)
-        return total
-
-    up, down = lax.optimization_barrier((add(4).astype(BF), add(-3).astype(BF)))
-    up, down = to_row(up, ring_z(1)), to_row(down, ring_z(-1))
+        return rest[k - 4 : k - 2].astype(F32) + theirs[k : k + 2].astype(F32)
+
     features_t = features.T
     for k in (3, 2, 1):
         here_up, here_down = add(k), (add(1 - k) if k > 1 else add(0))

time: 196 us -> 192 us (0.980)
  starting transfers between devices: 75.5 us -> 70.9 us
  waiting for transfers between devices: 51.7 us -> 47.6 us
  Pallas kernels: 26.3 us -> 29.3 us
    ppermute x28, waiting for transfers between devices: 30.9 us -> 23.2 us  [to_row(): return lax.ppermute(value, 'row', route)]
    ppermute x14, waiting for transfers between devices: 12.9 us -> 18.2 us  [to_col(): return lax.ppermute(value, 'col', route)]
    ppermute x14, starting transfers between devices: 24.6 us -> 19.3 us  [to_col(): return lax.ppermute(value, 'col', route)]
    pallas_call x2 -> x3, Pallas kernels: 12.4 us -> 15.4 us  [backward_part(): pl.pallas_call(functools.partial(backward_kernel, base), in_specs=[smem]...]
  transfers between devices with their start and end apart: 43 -> 43, of which waited for: 22 -> 23; matrix products, arithmetic and copies ran while one was open for 4% -> 5% of each run, Pallas kernels for 8% -> 10%
where the time goes in v2:
time: 192 us; the launch traced here: 191 us
  starting transfers between devices  70.9 us (37%)
  waiting for transfers between devices  47.6 us (25%)
  Pallas kernels  29.3 us (15%)
  blocking collectives  24 us (12%)
  other arithmetic  10.5 us (5%)
  local copies, waits for them, and re-layouts  5.19 us (3%)
  matrix products  2.6 us (1%)
    ppermute x28, starting transfers between devices, to_row(): return lax.ppermute(value, 'row', route)  47.8 us
    ppermute x28, waiting for transfers between devices, to_row(): return lax.ppermute(value, 'row', route)  23.2 us
    ppermute x14, starting transfers between devices, to_col(): return lax.ppermute(value, 'col', route)  19.3 us
    ppermute x14, waiting for transfers between devices, to_col(): return lax.ppermute(value, 'col', route)  18.2 us
    pallas_call x3, Pallas kernels, backward_part(): pl.pallas_call(functools.partial(backward_kernel, base), in_specs=[smem]...  15.4 us
    pallas_call x2, Pallas kernels, forward_part(): pl.pallas_call(functools.partial(forward_kernel, base, half, total is Non...  13.9 us
    all_to_all x1, blocking collectives, sum_everywhere(): lax.all_to_all(jnp.broadcast_to(part[None], (COLS,) + part.shape), 'col',...  12 us
    all_to_all x1, blocking collectives, sum_everywhere(): every = lax.all_to_all(every, 'row', 0, 0, axis_index_groups=groups)  12 us
  transfers between devices with their start and end apart: 43, of which 23 were waited for; matrix products, arithmetic and copies ran while one was open for 5% of the time, Pallas kernels for 10%

profile of v2, /device:TPU:1, one launch (start us, length us, event | category | flops | bytes accessed | tf_op | source)
XLA Modules:
  0.0 191.2 jit_solution(487610857792996361)
XLA Ops:
  9.9 4.0 %collective-permute-start.7 = (bf16[2,256,256]{2,1,0:T(8,128)(2,1)S(1)}, bf16[2,256,256]{2,1,0:T(8,128)(2,1)S(1)}, u32[]{:S(2)}, u32[]{:S(2)}) collective-permute-start(bf16[2,256,256]{2,1,0:T(8,128)(2,1)S(1)} %pad_maximum_fusion.1.refs_0_), channel_id=1, source_target_pairs={{0,112},{8,120},{16,0},{24,8},{32,16},{40,24},{48,32},{56,40},{64,... | collective-permute-start | bytes 786440 | tf_op jit(solution)/shard_map/ppermute | solution.py:33
  19.0 2.7 %collective-permute-start.10 = (bf16[2,256,256]{2,1,0:T(8,128)(2,1)S(1)}, bf16[2,256,256]{2,1,0:T(8,128)(2,1)S(1)}, u32[]{:S(2)}, u32[]{:S(2)}) collective-permute-start(bf16[2,256,256]{2,1,0:T(8,128)(2,1)S(1)} %collective-permute-done.7.refs_4_), channel_id=1, source_target_pairs={{0,112},{8,120},{16,0},{24,8},{32,16},{40,24},{48,32},{56,40},{64,... | collective-permute-start | bytes 786440 | tf_op jit(solution)/shard_map/ppermute | solution.py:33
  21.6 2.7 %collective-permute-start.5 = (bf16[2,256,256]{2,1,0:T(8,128)(2,1)S(1)}, bf16[2,256,256]{2,1,0:T(8,128)(2,1)S(1)}, u32[]{:S(2)}, u32[]{:S(2)}) collective-permute-start(bf16[2,256,256]{2,1,0:T(8,128)(2,1)S(1)} %pad_maximum_fusion.1.refs_0_), channel_id=1, source_target_pairs={{0,8},{8,0},{16,24},{24,16},{32,40},{40,32},{48,56},{56,48},{64,72... | collective-permute-start | bytes 786440 | tf_op jit(solution)/shard_map/ppermute | solution.py:33
  28.4 3.7 %collective-permute-start.8 = (bf16[2,256,256]{2,1,0:T(8,128)(2,1)S(1)}, bf16[2,256,256]{2,1,0:T(8,128)(2,1)S(1)}, u32[]{:S(2)}, u32[]{:S(2)}) collective-permute-start(bf16[2,256,256]{2,1,0:T(8,128)(2,1)S(1)} %collective-permute-done.7.refs_4_), channel_id=1, source_target_pairs={{0,8},{8,0},{16,24},{24,16},{32,40},{40,32},{48,56},{56,48},{64,72... | collective-permute-start | bytes 786440 | tf_op jit(solution)/shard_map/ppermute | solution.py:33
  32.6 3.8 %collective-permute-start.12 = (bf16[2,256,256]{2,1,0:T(8,128)(2,1)S(1)}, bf16[2,256,256]{2,1,0:T(8,128)(2,1)S(1)}, u32[]{:S(2)}, u32[]{:S(2)}) collective-permute-start(bf16[2,256,256]{2,1,0:T(8,128)(2,1)S(1)} %collective-permute-done.3.refs_10_), channel_id=1, source_target_pairs={{0,8},{8,0},{16,24},{24,16},{32,40},{40,32},{48,56},{56,48},{64,72... | collective-permute-start | bytes 786440 | tf_op jit(solution)/shard_map/ppermute | solution.py:33
  38.8 9.5 %shard_map.130.refs_2_ = f32[16,128,256]{2,1,0:T(8,128)} custom-call(s32[64]{0:T(128)} %fusion.16.blocks, s32[192]{0:T(256)} %get-tuple-element.55.rows, s32[192]{0:T(256)} %get-tuple-element.56.cols, bf16[32,6,128,128]{3,2,1,0:T(8,128)(2,1)} %bitcast.27, bf16[2,256,256]{2,1,0:T(8,128)(2,1)} %copy-done.9, bf16[2,256,256]{2,1,0:T(8,128)(2,1)} %copy-done.14, ...), custom_call_target="tpu_custom_call" | custom-call | flops 2818572288 | bytes 18874368 | tf_op jit(solution)/shard_map/pallas_call | solution.py:110
  50.9 4.4 %shard_map.131 = (f32[256,256]{1,0:T(8,128)}, bf16[256,256]{1,0:T(8,128)(2,1)}, bf16[256,256]{1,0:T(8,128)(2,1)}, bf16[256,256]{1,0:T(8,128)(2,1)}, bf16[256,256...) custom-call(s32[64]{0:T(128)} %fusion.16.blocks, ...), custom_call_target="tpu_custom_call" | custom-call | flops 402653184 | bytes 6291456 | tf_op jit(solution)/shard_map/pallas_call | solution.py:110
  55.3 2.8 %collective-permute-start.16 = (bf16[256,256]{1,0:T(8,128)(2,1)}, bf16[256,256]{1,0:T(8,128)(2,1)S(1)}, u32[]{:S(2)}, u32[]{:S(2)}) collective-permute-start(bf16[256,256]{1,0:T(8,128)(2,1)} %get-tuple-element.61), channel_id=1, source_target_pairs={{0,1},{1,0},{2,3},{3,2},{4,5},{5,4},{6,7},{7,6},{8,9},{9,8},{10,11... | collective-permute-start | bytes 393224 | tf_op jit(solution)/shard_map/ppermute | solution.py:37
  62.8 4.8 %collective-permute-start.21 = (bf16[256,256]{1,0:T(8,128)(2,1)}, bf16[256,256]{1,0:T(8,128)(2,1)S(1)}, u32[]{:S(2)}, u32[]{:S(2)}) collective-permute-start(bf16[256,256]{1,0:T(8,128)(2,1)} %get-tuple-element.66), channel_id=1, source_target_pairs={{0,7},{1,6},{2,1},{3,0},{4,3},{5,2},{6,5},{7,4},{8,15},{9,14},{10,... | collective-permute-start | bytes 393224 | tf_op jit(solution)/shard_map/ppermute | solution.py:37
  68.1 2.7 %collective-permute-done.20 = bf16[256,256]{1,0:T(8,128)(2,1)S(1)} collective-permute-done((bf16[256,256]{1,0:T(8,128)(2,1)}, bf16[256,256]{1,0:T(8,128)(2,1)S(1)}, u32[]{:S(2)}, u32[]{:S(2)}) %collective-permute-start.20) | collective-permute-done | bytes 131104 | tf_op jit(solution)/shard_map/ppermute | solution.py:37
  71.1 4.5 %collective-permute-done.22 = bf16[256,256]{1,0:T(8,128)(2,1)S(1)} collective-permute-done((bf16[256,256]{1,0:T(8,128)(2,1)}, bf16[256,256]{1,0:T(8,128)(2,1)S(1)}, u32[]{:S(2)}, u32[]{:S(2)}) %collective-permute-start.22) | collective-permute-done | bytes 131104 | tf_op jit(solution)/shard_map/ppermute | solution.py:37
  90.5 3.7 %collective-permute-done.30.refs_7_ = bf16[2,256,128]{2,1,0:T(8,128)(2,1)S(1)} collective-permute-done((bf16[2,256,128]{2,1,0:T(8,128)(2,1)S(1)}, bf16[2,256,128]{2,1,0:T(8,128)(2,1)S(1)}, u32[]{:S(2)}, u32[]{:S(2)}) %collective-permute-start.30) | collective-permute-done | bytes 131104 | tf_op jit(solution)/shard_map/ppermute | solution.py:37
  94.9 6.2 %shard_map.132 = bf16[16,256,256]{2,1,0:T(8,128)(2,1)} custom-call(s32[64]{0:T(128)} %fusion.16.blocks, s32[192]{0:T(256)} %get-tuple-element.55.rows, s32[192]{0:T(256)} %get-tuple-element.56.cols, bf16[32,6,128,128]{3,2,1,0:T(8,128)(2,1)} %bitcast.29, bf16[2,256,128]{2,1,0:T(8,128)(2,1)} %bitcast.36, bf16[2,256,128]{2,1,0:T(8,128)(2,1)} %copy-done.2, ...), custom_call_target="tpu_custom_call" | custom-call | flops 1610612736 | bytes 9437184 | tf_op jit(solution)/shard_map/pallas_call | solution.py:166
  103.1 3.7 %shard_map.133 = bf16[4,256,256]{2,1,0:T(8,128)(2,1)} custom-call(s32[64]{0:T(128)} %fusion.16.blocks, s32[192]{0:T(256)} %get-tuple-element.55.rows, s32[192]{0:T(256)} %get-tuple-element.56.cols, bf16[32,6,128,128]{3,2,1,0:T(8,128)(2,1)} %bitcast.30, bf16[2,256,128]{2,1,0:T(8,128)(2,1)} %bitcast.37, bf16[2,256,128]{2,1,0:T(8,128)(2,1)} %copy-done.2, ...), custom_call_target="tpu_custom_call" | custom-call | flops 402653184 | bytes 3145728 | tf_op jit(solution)/shard_map/pallas_call | solution.py:166
  111.1 5.5 %shard_map.134 = bf16[12,256,256]{2,1,0:T(8,128)(2,1)} custom-call(s32[64]{0:T(128)} %fusion.16.blocks, s32[192]{0:T(256)} %get-tuple-element.55.rows, s32[192]{0:T(256)} %get-tuple-element.56.cols, bf16[32,6,128,128]{3,2,1,0:T(8,128)(2,1)} %bitcast.31, bf16[2,256,128]{2,1,0:T(8,128)(2,1)} %bitcast.38, bf16[2,256,128]{2,1,0:T(8,128)(2,1)} %copy-done.2, ...), custom_call_target="tpu_custom_call" | custom-call | flops 1207959552 | bytes 7340032 | tf_op jit(solution)/shard_map/pallas_call | solution.py:166
  122.1 5.3 %collective-permute-done.34 = bf16[2,256,256]{2,1,0:T(8,128)(2,1)S(1)} collective-permute-done((bf16[2,256,256]{2,1,0:T(8,128)(2,1)S(1)}, bf16[2,256,256]{2,1,0:T(8,128)(2,1)S(1)}, u32[]{:S(2)}, u32[]{:S(2)}) %collective-permute-start.34) | collective-permute-done | bytes 262176 | tf_op jit(solution)/shard_map/ppermute | solution.py:33
  130.3 4.4 %collective-permute-done.36 = bf16[2,256,256]{2,1,0:T(8,128)(2,1)S(1)} collective-permute-done((bf16[2,256,256]{2,1,0:T(8,128)(2,1)S(1)}, bf16[2,256,256]{2,1,0:T(8,128)(2,1)S(1)}, u32[]{:S(2)}, u32[]{:S(2)}) %collective-permute-start.36) | collective-permute-done | bytes 262176 | tf_op jit(solution)/shard_map/ppermute | solution.py:33
  137.2 4.1 %collective-permute-done.38 = bf16[2,256,256]{2,1,0:T(8,128)(2,1)S(1)} collective-permute-done((bf16[2,256,256]{2,1,0:T(8,128)(2,1)S(1)}, bf16[2,256,256]{2,1,0:T(8,128)(2,1)S(1)}, u32[]{:S(2)}, u32[]{:S(2)}) %collective-permute-start.38) | collective-permute-done | bytes 262176 | tf_op jit(solution)/shard_map/ppermute | solution.py:33
  143.0 4.3 %collective-permute-start.39 = (f32[320,256]{1,0:T(8,128)S(1)}, f32[320,256]{1,0:T(8,128)S(1)}, u32[]{:S(2)}, u32[]{:S(2)}) collective-permute-start(f32[320,256]{1,0:T(8,128)S(1)} %slice_select_fusion), channel_id=1, source_target_pairs={{0,8},{8,0},{16,24},{24,16},{32,40},{40,32},{48,56},{56,48},{64,72... | collective-permute-start | bytes 983048 | tf_op jit(solution)/shard_map/ppermute | solution.py:33
  149.2 3.8 %all-to-all-start = ((bf16[8,40,256]{2,1,0:T(8,128)(2,1)}), bf16[8,40,256]{2,1,0:T(8,128)(2,1)S(1)}, u32[]{:S(2)}, u32[]{:S(2)}) async-start(bf16[8,40,256]{2,1,0:T(8,128)(2,1)} %bitcast.9), calls=%async_computation | async-start | bytes 327680 | tf_op jit(solution)/shard_map/all_to_all | solution.py:191
  154.0 6.2 %all-to-all-done = bf16[8,40,256]{2,1,0:T(8,128)(2,1)S(1)} async-done(((bf16[8,40,256]{2,1,0:T(8,128)(2,1)}), bf16[8,40,256]{2,1,0:T(8,128)(2,1)S(1)}, u32[]{:S(2)}, u32[]{:S(2)}) %all-to-all-start) | async-done | bytes 163872 | tf_op jit(solution)/shard_map/all_to_all | solution.py:191
  160.3 12.0 %all_to_all.15 = bf16[16,40,256]{2,1,0:T(8,128)(2,1)S(1)} all-to-all(bf16[16,40,256]{2,1,0:T(8,128)(2,1)S(1)} %broadcast_in_dim.6), channel_id=1, replica_groups={{0,16,32,48,64,80,96,112,128,144,160,176,192,208,224,240},{8,24,40,56,7..., dimensions={0} | all-to-all | bytes 655360 | tf_op jit(solution)/shard_map/all_to_all | solution.py:196
  172.3 12.0 %all_to_all.16 = f32[8,40,256]{2,1,0:T(8,128)S(1)} all-to-all(f32[8,40,256]{2,1,0:T(8,128)S(1)} %broadcast_in_dim.7), channel_id=1, replica_groups=mesh['row'=32,'col'=8] {'col'}, dimensions={0} | all-to-all | bytes 655360 | tf_op jit(solution)/shard_map/all_to_all | solution.py:198
  184.3 4.7 %collective-permute-start.41 = (f32[320,256]{1,0:T(8,128)S(1)}, f32[320,256]{1,0:T(8,128)S(1)}, u32[]{:S(2)}, u32[]{:S(2)}) collective-permute-start(f32[320,256]{1,0:T(8,128)S(1)} %bitcast.39), channel_id=1, source_target_pairs={{0,8},{8,0},{16,24},{24,16},{32,40},{40,32},{48,56},{56,48},{64,72... | collective-permute-start | bytes 983048 | tf_op jit(solution)/shard_map/ppermute | solution.py:33
  (159 shorter events, 68.7 us)
Async XLA Ops:
  7.4 11.5 %collective-permute-start.1 = (bf16[2,256,256]{2,1,0:T(8,128)(2,1)S(1)}, bf16[2,256,256]{2,1,0:T(8,128)(2,1)S(1)}, u32[]{:S(2)}, u32[]{:S(2)}) collective-permute-start(bf16[2,256,256]{2,1,0:T(8,128)(2,1)S(1)} %pad_maximum_fusion.1.refs_0_), channel_id=1, source_target_pairs={{0,16},{8,24},{16,32},{24,40},{32,48},{40,56},{48,64},{56,72},{64,... | collective-permute-start | bytes 786440 | tf_op jit(solution)/shard_map/ppermute | solution.py:33
  9.9 9.0 %collective-permute-start.7 = (bf16[2,256,256]{2,1,0:T(8,128)(2,1)S(1)}, bf16[2,256,256]{2,1,0:T(8,128)(2,1)S(1)}, u32[]{:S(2)}, u32[]{:S(2)}) collective-permute-start(bf16[2,256,256]{2,1,0:T(8,128)(2,1)S(1)} %pad_maximum_fusion.1.refs_0_), channel_id=1, source_target_pairs={{0,112},{8,120},{16,0},{24,8},{32,16},{40,24},{48,32},{56,40},{64,... | collective-permute-start | bytes 786440 | tf_op jit(solution)/shard_map/ppermute | solution.py:33
  18.9 6.8 %collective-permute-start.2 = (bf16[2,256,256]{2,1,0:T(8,128)(2,1)S(1)}, bf16[2,256,256]{2,1,0:T(8,128)(2,1)S(1)}, u32[]{:S(2)}, u32[]{:S(2)}) collective-permute-start(bf16[2,256,256]{2,1,0:T(8,128)(2,1)S(1)} %collective-permute-done.1.refs_2_), channel_id=1, source_target_pairs={{0,16},{8,24},{16,32},{24,40},{32,48},{40,56},{48,64},{56,72},{64,... | collective-permute-start | bytes 786440 | tf_op jit(solution)/shard_map/ppermute | solution.py:33
  19.0 6.8 %collective-permute-start.10 = (bf16[2,256,256]{2,1,0:T(8,128)(2,1)S(1)}, bf16[2,256,256]{2,1,0:T(8,128)(2,1)S(1)}, u32[]{:S(2)}, u32[]{:S(2)}) collective-permute-start(bf16[2,256,256]{2,1,0:T(8,128)(2,1)S(1)} %collective-permute-done.7.refs_4_), channel_id=1, source_target_pairs={{0,112},{8,120},{16,0},{24,8},{32,16},{40,24},{48,32},{56,40},{64,... | collective-permute-start | bytes 786440 | tf_op jit(solution)/shard_map/ppermute | solution.py:33
  21.6 10.5 %collective-permute-start.5 = (bf16[2,256,256]{2,1,0:T(8,128)(2,1)S(1)}, bf16[2,256,256]{2,1,0:T(8,128)(2,1)S(1)}, u32[]{:S(2)}, u32[]{:S(2)}) collective-permute-start(bf16[2,256,256]{2,1,0:T(8,128)(2,1)S(1)} %pad_maximum_fusion.1.refs_0_), channel_id=1, source_target_pairs={{0,8},{8,0},{16,24},{24,16},{32,40},{40,32},{48,56},{56,48},{64,72... | collective-permute-start | bytes 786440 | tf_op jit(solution)/shard_map/ppermute | solution.py:33
  24.4 7.8 %collective-permute-start.6 = (bf16[2,256,256]{2,1,0:T(8,128)(2,1)S(1)}, bf16[2,256,256]{2,1,0:T(8,128)(2,1)S(1)}, u32[]{:S(2)}, u32[]{:S(2)}) collective-permute-start(bf16[2,256,256]{2,1,0:T(8,128)(2,1)S(1)} %collective-permute-done.1.refs_2_), channel_id=1, source_target_pairs={{0,8},{8,0},{16,24},{24,16},{32,40},{40,32},{48,56},{56,48},{64,72... | collective-permute-start | bytes 786440 | tf_op jit(solution)/shard_map/ppermute | solution.py:33
  25.8 6.9 %collective-permute-start.3 = (bf16[2,256,256]{2,1,0:T(8,128)(2,1)S(1)}, bf16[2,256,256]{2,1,0:T(8,128)(2,1)S(1)}, u32[]{:S(2)}, u32[]{:S(2)}) collective-permute-start(bf16[2,256,256]{2,1,0:T(8,128)(2,1)S(1)} %collective-permute-done.2.refs_6_), channel_id=1, source_target_pairs={{0,16},{8,24},{16,32},{24,40},{32,48},{40,56},{48,64},{56,72},{64,... | collective-permute-start | bytes 786440 | tf_op jit(solution)/shard_map/ppermute | solution.py:33
  25.8 10.7 %collective-permute-start.13 = (bf16[2,256,256]{2,1,0:T(8,128)(2,1)S(1)}, bf16[2,256,256]{2,1,0:T(8,128)(2,1)S(1)}, u32[]{:S(2)}, u32[]{:S(2)}) collective-permute-start(bf16[2,256,256]{2,1,0:T(8,128)(2,1)S(1)} %collective-permute-done.10.refs_8_), channel_id=1, source_target_pairs={{0,112},{8,120},{16,0},{24,8},{32,16},{40,24},{48,32},{56,40},{64,... | collective-permute-start | bytes 786440 | tf_op jit(solution)/shard_map/ppermute | solution.py:33
  28.4 8.1 %collective-permute-start.8 = (bf16[2,256,256]{2,1,0:T(8,128)(2,1)S(1)}, bf16[2,256,256]{2,1,0:T(8,128)(2,1)S(1)}, u32[]{:S(2)}, u32[]{:S(2)}) collective-permute-start(bf16[2,256,256]{2,1,0:T(8,128)(2,1)S(1)} %collective-permute-done.7.refs_4_), channel_id=1, source_target_pairs={{0,8},{8,0},{16,24},{24,16},{32,40},{40,32},{48,56},{56,48},{64,72... | collective-permute-start | bytes 786440 | tf_op jit(solution)/shard_map/ppermute | solution.py:33
  36.6 11.8 %collective-permute-start.4 = (bf16[2,256,256]{2,1,0:T(8,128)(2,1)S(1)}, bf16[2,256,256]{2,1,0:T(8,128)(2,1)S(1)}, u32[]{:S(2)}, u32[]{:S(2)}) collective-permute-start(bf16[2,256,256]{2,1,0:T(8,128)(2,1)S(1)} %collective-permute-done.3.refs_10_), channel_id=1, source_target_pairs={{0,16},{8,24},{16,32},{24,40},{32,48},{40,56},{48,64},{56,72},{64,... | collective-permute-start | bytes 786440 | tf_op jit(solution)/shard_map/ppermute | solution.py:33
  55.3 7.6 %collective-permute-start.16 = (bf16[256,256]{1,0:T(8,128)(2,1)}, bf16[256,256]{1,0:T(8,128)(2,1)S(1)}, u32[]{:S(2)}, u32[]{:S(2)}) collective-permute-start(bf16[256,256]{1,0:T(8,128)(2,1)} %get-tuple-element.61), channel_id=1, source_target_pairs={{0,1},{1,0},{2,3},{3,2},{4,5},{5,4},{6,7},{7,6},{8,9},{9,8},{10,11... | collective-permute-start | bytes 393224 | tf_op jit(solution)/shard_map/ppermute | solution.py:37
  58.1 9.5 %collective-permute-start.17 = (bf16[256,256]{1,0:T(8,128)(2,1)}, bf16[256,256]{1,0:T(8,128)(2,1)S(1)}, u32[]{:S(2)}, u32[]{:S(2)}) collective-permute-start(bf16[256,256]{1,0:T(8,128)(2,1)} %get-tuple-element.62), channel_id=1, source_target_pairs={{0,2},{1,3},{2,4},{3,5},{4,6},{5,7},{6,0},{7,1},{8,10},{9,11},{10,... | collective-permute-start | bytes 393224 | tf_op jit(solution)/shard_map/ppermute | solution.py:37
  59.4 8.2 %collective-permute-start.18 = (bf16[256,256]{1,0:T(8,128)(2,1)}, bf16[256,256]{1,0:T(8,128)(2,1)S(1)}, u32[]{:S(2)}, u32[]{:S(2)}) collective-permute-start(bf16[256,256]{1,0:T(8,128)(2,1)} %get-tuple-element.63), channel_id=1, source_target_pairs={{0,6},{1,7},{2,0},{3,1},{4,2},{5,3},{6,4},{7,5},{8,14},{9,15},{10,... | collective-permute-start | bytes 393224 | tf_op jit(solution)/shard_map/ppermute | solution.py:37
  60.9 7.2 %collective-permute-start.19 = (bf16[256,256]{1,0:T(8,128)(2,1)}, bf16[256,256]{1,0:T(8,128)(2,1)S(1)}, u32[]{:S(2)}, u32[]{:S(2)}) collective-permute-start(bf16[256,256]{1,0:T(8,128)(2,1)} %get-tuple-element.64), channel_id=1, source_target_pairs={{0,4},{1,5},{2,6},{3,7},{4,0},{5,1},{6,2},{7,3},{8,12},{9,13},{10,... | collective-permute-start | bytes 393224 | tf_op jit(solution)/shard_map/ppermute | solution.py:37
  62.5 8.2 %collective-permute-start.20 = (bf16[256,256]{1,0:T(8,128)(2,1)}, bf16[256,256]{1,0:T(8,128)(2,1)S(1)}, u32[]{:S(2)}, u32[]{:S(2)}) collective-permute-start(bf16[256,256]{1,0:T(8,128)(2,1)} %get-tuple-element.65), channel_id=1, source_target_pairs={{0,3},{1,2},{2,5},{3,4},{4,7},{5,6},{6,1},{7,0},{8,11},{9,10},{10,... | collective-permute-start | bytes 393224 | tf_op jit(solution)/shard_map/ppermute | solution.py:37
  62.8 8.2 %collective-permute-start.21 = (bf16[256,256]{1,0:T(8,128)(2,1)}, bf16[256,256]{1,0:T(8,128)(2,1)S(1)}, u32[]{:S(2)}, u32[]{:S(2)}) collective-permute-start(bf16[256,256]{1,0:T(8,128)(2,1)} %get-tuple-element.66), channel_id=1, source_target_pairs={{0,7},{1,6},{2,1},{3,0},{4,3},{5,2},{6,5},{7,4},{8,15},{9,14},{10,... | collective-permute-start | bytes 393224 | tf_op jit(solution)/shard_map/ppermute | solution.py:37
  67.6 7.9 %collective-permute-start.22 = (bf16[256,256]{1,0:T(8,128)(2,1)}, bf16[256,256]{1,0:T(8,128)(2,1)S(1)}, u32[]{:S(2)}, u32[]{:S(2)}) collective-permute-start(bf16[256,256]{1,0:T(8,128)(2,1)} %get-tuple-element.67), channel_id=1, source_target_pairs={{0,5},{1,4},{2,7},{3,6},{4,1},{5,0},{6,3},{7,2},{8,13},{9,12},{10,... | collective-permute-start | bytes 393224 | tf_op jit(solution)/shard_map/ppermute | solution.py:37
  84.7 9.5 %collective-permute-start.30 = (bf16[2,256,128]{2,1,0:T(8,128)(2,1)S(1)}, bf16[2,256,128]{2,1,0:T(8,128)(2,1)S(1)}, u32[]{:S(2)}, u32[]{:S(2)}) collective-permute-start(bf16[2,256,128]{2,1,0:T(8,128)(2,1)S(1)} %collective-permute-done.24.refs_1_), channel_id=1, source_target_pairs={{0,2},{1,3},{2,4},{3,5},{4,6},{5,7},{6,0},{7,1},{8,10},{9,11},{10,... | collective-permute-start | bytes 393224 | tf_op jit(solution)/shard_map/ppermute | solution.py:37
  108.3 9.9 %collective-permute-start.32 = (bf16[2,256,256]{2,1,0:T(8,128)(2,1)S(1)}, bf16[2,256,256]{2,1,0:T(8,128)(2,1)S(1)}, u32[]{:S(2)}, u32[]{:S(2)}) collective-permute-start(bf16[2,256,256]{2,1,0:T(8,128)(2,1)S(1)} %get-tuple-element.77), channel_id=1, source_target_pairs={{0,16},{8,24},{16,32},{24,40},{32,48},{40,56},{48,64},{56,72},{64,... | collective-permute-start | bytes 786440 | tf_op jit(solution)/shard_map/ppermute | solution.py:33
  109.0 9.2 %collective-permute-start.33 = (bf16[2,256,256]{2,1,0:T(8,128)(2,1)S(1)}, bf16[2,256,256]{2,1,0:T(8,128)(2,1)}, u32[]{:S(2)}, u32[]{:S(2)}) collective-permute-start(bf16[2,256,256]{2,1,0:T(8,128)(2,1)S(1)} %get-tuple-element.78), channel_id=1, source_target_pairs={{0,112},{8,120},{16,0},{24,8},{32,16},{40,24},{48,32},{56,40},{64,... | collective-permute-start | bytes 786440 | tf_op jit(solution)/shard_map/ppermute | solution.py:33
  119.4 8.0 %collective-permute-start.34 = (bf16[2,256,256]{2,1,0:T(8,128)(2,1)S(1)}, bf16[2,256,256]{2,1,0:T(8,128)(2,1)S(1)}, u32[]{:S(2)}, u32[]{:S(2)}) collective-permute-start(bf16[2,256,256]{2,1,0:T(8,128)(2,1)S(1)} %add_convert_fusion.5), channel_id=1, source_target_pairs={{0,16},{8,24},{16,32},{24,40},{32,48},{40,56},{48,64},{56,72},{64,... | collective-permute-start | bytes 786440 | tf_op jit(solution)/shard_map/ppermute | solution.py:33
  120.4 7.0 %collective-permute-start.35 = (bf16[2,256,256]{2,1,0:T(8,128)(2,1)S(1)}, bf16[2,256,256]{2,1,0:T(8,128)(2,1)S(1)}, u32[]{:S(2)}, u32[]{:S(2)}) collective-permute-start(bf16[2,256,256]{2,1,0:T(8,128)(2,1)S(1)} %add_convert_fusion.4), channel_id=1, source_target_pairs={{0,112},{8,120},{16,0},{24,8},{32,16},{40,24},{48,32},{56,40},{64,... | collective-permute-start | bytes 786440 | tf_op jit(solution)/shard_map/ppermute | solution.py:33
  127.6 7.1 %collective-permute-start.36 = (bf16[2,256,256]{2,1,0:T(8,128)(2,1)S(1)}, bf16[2,256,256]{2,1,0:T(8,128)(2,1)S(1)}, u32[]{:S(2)}, u32[]{:S(2)}) collective-permute-start(bf16[2,256,256]{2,1,0:T(8,128)(2,1)S(1)} %add_convert_fusion.3), channel_id=1, source_target_pairs={{0,16},{8,24},{16,32},{24,40},{32,48},{40,56},{48,64},{56,72},{64,... | collective-permute-start | bytes 786440 | tf_op jit(solution)/shard_map/ppermute | solution.py:33
  149.2 11.0 %all-to-all-start = ((bf16[8,40,256]{2,1,0:T(8,128)(2,1)}), bf16[8,40,256]{2,1,0:T(8,128)(2,1)S(1)}, u32[]{:S(2)}, u32[]{:S(2)}) async-start(bf16[8,40,256]{2,1,0:T(8,128)(2,1)} %bitcast.9), calls=%async_computation | async-start | bytes 327680 | tf_op jit(solution)/shard_map/all_to_all | solution.py:191
  (47 other events, 360.6 us)
